TPU v7x, 32 devices: a whole 2x2x4 slice. The times are simulated.
32 devices in a mesh: groups: 2 (over y), seq: 16 (over z, x, core).
Axes of the slice: x: 2, y: 2, z: 4, core: 2. Of those that a mesh axis runs over, the one named last changes fastest.
Arguments:
- q_fresh: bfloat16 [2048, 5120], P(('groups', 'seq')), parts along dimension 0, may hold values from -48 to 48
- k_fresh: bfloat16 [2048, 5120], P(('groups', 'seq')), parts along dimension 0, may hold values from -48 to 48
- v_fresh: bfloat16 [2048, 5120], P(('groups', 'seq')), parts along dimension 0, may hold values from -6 to 6
- q_gain: bfloat16 [5120], replicated, may hold values from 1 to 4
- k_gain: bfloat16 [5120], replicated, may hold values from 0.5 to 2
- stale_keys: bfloat16 [32, 512, 640], P(('groups', 'seq')), parts along dimension 0, may hold values from -6 to 6
- stale_values: bfloat16 [32, 512, 640], P(('groups', 'seq')), parts along dimension 0, may hold values from -6 to 6
- gate_table: bfloat16 [50, 5120], replicated, may hold values from 0.5 to 3
- assign: int32 [32], P('groups'), parts along dimension 0, may hold values from 0 to 15, each once
- counts: int32 [32], P('groups'), parts along dimension 0, may hold values from 1 to 64, 768 in all
- timestep: int32 [2], P('groups'), parts along dimension 0, may hold values from 0 to 49
Outputs:
- mixed: bfloat16 [2048, 5120], P(('groups', 'seq')), parts along dimension 0
- new_keys: bfloat16 [32, 512, 640], P(('groups', 'seq')), parts along dimension 0
- new_values: bfloat16 [32, 512, 640], P(('groups', 'seq')), parts along dimension 0
There are 2 independent parts, one for each index of `groups`. A program takes and returns all parts, laid end to end along the dimension named above; an argument that names none is the same for every part. Nothing has to cross between parts.
Inputs may be any that keep to these rules, and one draw needn't show every extreme that they name: Index i of seq holds the rows of patch assign[i]; every patch is held once. `counts`: some patch has all 64 tokens live.
All inputs are finite; a program needn't handle non-finite values.
Results may differ from a plain program's by a relative error of at most 0.011.
Values may be sent and summed in bfloat16 or wider, within the bound.
No kernel may reach another device: no remote copies, remote signals or barrier semaphores. Data moves between devices by JAX's collectives and lax.ppermute only.
A program may use at most 64 MiB of HBM per device.

v0:
```python
import functools
import math

import jax
import jax.numpy as jnp
import numpy as np
from jax import lax
from jax.experimental import pallas as pl
from jax.experimental.pallas import tpu as pltpu
from jax.sharding import PartitionSpec as P

HEAD = 128
RMS_EPS = 1e-06
VMEM_BYTES = 32 * 1024 * 1024
SMEM, VMEM = pltpu.SMEM, pltpu.VMEM


def call(kernel, name, ins, outs, flops, n_bytes, scratch=()):
    shapes = [jax.ShapeDtypeStruct(shape, dtype) for _, shape, dtype in outs]
    return pl.pallas_call(
        kernel,
        out_shape=shapes,
        in_specs=[pl.BlockSpec(memory_space=m) for m in ins],
        out_specs=[pl.BlockSpec(memory_space=m) for m, _, _ in outs],
        scratch_shapes=scratch,
        compiler_params=pltpu.CompilerParams(vmem_limit_bytes=VMEM_BYTES),
        cost_estimate=pl.CostEstimate(flops=flops, bytes_accessed=n_bytes, transcendentals=0),
        name=name,
    )


def to_partner(value, distance, size):
    if distance == 0:
        return value
    return lax.ppermute(value, "seq", [(i, i ^ distance) for i in range(size)])


def to_block(value, distance, size):
    return lax.ppermute(value, "seq", [(i, (i + distance) % size) for i in range(size)])


def column(h):
    return slice(h * HEAD, (h + 1) * HEAD)


def place(slots):
    device = lax.axis_index("seq")
    return lax.rem(device, slots), lax.div(device, slots)


def live_of(assign, counts, index):
    return counts[assign[index]]


def live_lanes(assign, counts, tok, indices):
    width = tok * len(indices)
    lane = lax.broadcasted_iota(jnp.int32, (1, width), 1)
    count = jnp.zeros((1, width), jnp.int32)
    for i, index in enumerate(indices):
        count = jnp.where(lane // tok == i, live_of(assign, counts, index), count)
    return lane % tok, count


def choose_kernel(slots, blocks, sizes, assign, counts, out):
    most = jnp.int32(0)
    for b in range(blocks):
        total = jnp.int32(0)
        for i in range(slots):
            total = total + live_of(assign, counts, b * slots + i)
        most = jnp.maximum(most, total)
    which = jnp.int32(0)
    for n in sizes[:-1]:
        which = which + (most > n).astype(jnp.int32)
    out[0] = which


def compact_kernel(slots, tok, assign, counts, keys, values, out):
    rows, width, wide = out.shape[0], slots * tok, keys.shape[2]
    _, block = place(slots)
    indices = [block * slots + i for i in range(slots)]
    within, count = live_lanes(assign, counts, tok, indices)
    lane = lax.broadcasted_iota(jnp.int32, (1, width), 1)
    ahead = jnp.zeros((1, width), jnp.int32)
    for i, index in enumerate(indices):
        ahead = ahead + jnp.where(lane // tok > i, live_of(assign, counts, index), 0)
    goal = jnp.where(within < count, ahead + within, -1)
    row = lax.broadcasted_iota(jnp.int32, (rows, width), 0)
    pick = jnp.where(row == goal, 1.0, 0.0).astype(jnp.bfloat16)
    for part, ref in enumerate((keys, values)):
        moved = jnp.dot(pick, ref[0], preferred_element_type=jnp.float32)
        out[:, part * wide : (part + 1) * wide] = moved.astype(jnp.bfloat16)


def norm_kernel(slots, order, heads, assign, q, k, v, q_gain, k_gain, steps, *outs):
    tok, width = q.shape
    slot, block = place(slots)
    patch = assign[block * slots + slot]
    position = patch * tok + lax.broadcasted_iota(jnp.int32, (tok, HEAD), 0)
    angles = position.astype(jnp.float32) * steps[...]
    low = lax.broadcasted_iota(jnp.int32, (tok, HEAD), 1) < HEAD // 2
    cos_part = jnp.cos(angles)
    sin_part = jnp.sin(angles)
    sin_part = jnp.where(low, -sin_part, sin_part)

    def inverse(ref):
        total = jnp.zeros((tok, HEAD), jnp.float32)
        for c in range(0, width, HEAD):
            x = ref[:, c : c + HEAD].astype(jnp.float32)
            total = total + x * x
        return lax.rsqrt(jnp.sum(total, axis=1, keepdims=True) / width + RMS_EPS)

    scales = inverse(q), inverse(k)
    wide = heads * HEAD

    def one_head(h, _):
        to = pl.ds(pl.multiple_of(h * HEAD, HEAD), HEAD)
        for out, d in zip(outs, order):
            start = jnp.bitwise_xor(slot, d) * wide + h * HEAD
            col = pl.ds(pl.multiple_of(start, HEAD), HEAD)
            out[2 * tok : 3 * tok, to] = v[:, col]
            for part, (ref, gain) in enumerate(((q, q_gain), (k, k_gain))):
                x = ref[:, col].astype(jnp.float32) * scales[part]
                x = x * gain[:, col].astype(jnp.float32)
                turned = x * cos_part + pltpu.roll(x, HEAD // 2, 1) * sin_part
                out[part * tok : (part + 1) * tok, to] = turned.astype(jnp.bfloat16)
        return 0

    lax.fori_loop(0, heads, one_head, 0)


def cache_kernel(order, tok, *refs):
    new_keys, new_values = refs[len(order) :]
    slot, _ = place(len(order))
    for ref, d in zip(refs, order):
        at = pl.ds(pl.multiple_of(jnp.bitwise_xor(slot, d) * tok, tok), tok)
        new_keys[0, at, :] = ref[tok : 2 * tok, :]
        new_values[0, at, :] = ref[2 * tok : 3 * tok, :]


def attend(queries, sources, state):
    scale = HEAD**-0.5 / math.log(2.0)
    scores = [
        lax.dot_general(
            queries, keys, (((1,), (1,)), ((), ())), preferred_element_type=jnp.float32
        )
        + bias
        for keys, _, bias in sources
    ]
    tops = [jnp.max(s, axis=1, keepdims=True) for s in scores]
    top = functools.reduce(jnp.maximum, tops + ([] if state is None else [state[0]]))
    weights = [jnp.exp2(s * scale - top * scale) for s in scores]
    total = sum(jnp.sum(w, axis=1, keepdims=True) for w in weights)
    summed = sum(
        jnp.dot(w.astype(jnp.bfloat16), values, preferred_element_type=jnp.float32)
        for w, (_, values, _) in zip(weights, sources)
    )
    if state is not None:
        fading = jnp.exp2((state[0] - top) * scale)
        total = total + state[1] * fading
        summed = summed + state[2] * fading
    return top, total, summed


def store_state(stats, sums, parts):
    rows = parts[0][0].shape[0]
    lane = lax.broadcasted_iota(jnp.int32, (rows, HEAD), 1)
    packed = jnp.zeros((rows, HEAD), jnp.float32)
    for h, (top, total, summed) in enumerate(parts):
        packed = jnp.where(lane == h, top, packed)
        packed = jnp.where(lane == HEAD // 2 + h, total, packed)
        sums[:, column(h)] = summed
    stats[...] = packed


def load_state(stats, sums, h):
    half = HEAD // 2
    return stats[:, h : h + 1], stats[:, half + h : half + h + 1], sums[:, column(h)]


def attend_kernel(order, tok, blocks, heads, looped, step, n_state, assign, counts, *refs):
    slots = len(order)
    bundles, refs = refs[:slots], refs[slots:]
    stale, state, rest = refs[0], refs[1 : 1 + n_state], refs[1 + n_state :]
    final = step == blocks - 1
    slot, block = place(slots)
    source = lax.rem(block - step + blocks, blocks) * slots
    live = jnp.int32(0)
    for i in range(slots):
        live = live + live_of(assign, counts, source + i)
    lane = lax.broadcasted_iota(jnp.int32, (1, stale.shape[0]), 1)
    stale_bias = jnp.where(lane < live, 0.0, -jnp.inf)
    if final:
        gate, outs = rest[0], rest[1:]
        indices = [block * slots + jnp.bitwise_xor(slot, d) for d in order]
        within, count = live_lanes(assign, counts, tok, indices)
        fresh_bias = jnp.where(within < count, 0.0, -jnp.inf)

    def fresh(part, cols):
        return jnp.concatenate([r[part * tok : (part + 1) * tok, cols] for r in bundles], axis=0)

    def one_head(h):
        cols, past = [
            pl.ds(pl.multiple_of(c * HEAD, HEAD), HEAD) if looped else column(c)
            for c in (h, heads + h)
        ]
        sources = [(stale[:, cols], stale[:, past], stale_bias)]
        if final:
            sources.append((fresh(1, cols), fresh(2, cols), fresh_bias))
        before = load_state(*state, h) if state else None
        _, total, summed = result = attend(fresh(0, cols), sources, before)
        if final:
            rounded = (summed / total).astype(jnp.bfloat16).astype(jnp.float32)
            gated = (rounded * gate[:, cols].astype(jnp.float32)).astype(jnp.bfloat16)
            for i, out in enumerate(outs):
                out[:, cols] = gated[i * tok : (i + 1) * tok]
        return result

    if looped:
        lax.fori_loop(0, heads, lambda h, _: one_head(h) and 0, 0)
        return
    parts = [one_head(h) for h in range(heads)]
    if not final:
        store_state(*rest, parts)


def collect_kernel(order, heads, *refs):
    wide = heads * HEAD
    slot, _ = place(len(order))
    for ref, d in zip(refs, order):
        start = jnp.bitwise_xor(slot, d) * wide
        refs[-1][:, pl.ds(pl.multiple_of(start, wide), wide)] = ref[...]


def body(
    q_fresh,
    k_fresh,
    v_fresh,
    q_gain,
    k_gain,
    stale_keys,
    stale_values,
    gate_table,
    assign,
    counts,
    timestep,
):
    bf16, f32, i32 = jnp.bfloat16, jnp.float32, jnp.int32
    device = lax.axis_index("seq")
    size = lax.axis_size("seq")
    tok, model_width = q_fresh.shape
    block_rows, wide = stale_keys.shape[1:]
    slots = model_width // wide
    blocks = size // slots
    heads = wide // HEAD
    order = [6, 4, 7, 5, 2, 3, 1, 0]
    sizes = [block_rows * n // 32 for n in (26, 28, 32)] if blocks == 2 else [block_rows]
    rare = sizes[2:]

    (which,) = call(
        functools.partial(choose_kernel, slots, blocks, sizes),
        "choose",
        [SMEM] * 2,
        [(SMEM, (1,), i32)],
        0,
        8 * (block_rows * wide + tok * model_width),
    )(assign, counts)

    halves = np.arange(HEAD, dtype=np.float64) % (HEAD // 2)
    steps = jnp.asarray((10000.0 ** (-2.0 * halves / HEAD)).astype(np.float32)[None])

    def exchange(arrays, order):
        return [to_partner(a, d, size) for a, d in zip(arrays, order)]

    def run(rows, operands):
        assign, counts, keys, values, q, k, v, q_gain, k_gain, gate_table, timestep = operands
        (packed,) = call(
            functools.partial(compact_kernel, slots, tok),
            "compact",
            [SMEM] * 2 + [VMEM] * 2,
            [(VMEM, (rows, 2 * wide), bf16)],
            4 * rows * block_rows * wide,
            4 * (rows + block_rows) * wide,
        )(assign, counts, keys, values)
        stale = [to_block(packed, s * slots, size) for s in range(1, blocks)]
        bundles = []
        for part in (order[: slots // 2], order[slots // 2 :]):
            bundles += call(
                functools.partial(norm_kernel, slots, part, heads),
                "norm",
                [SMEM] + [VMEM] * 6,
                [(VMEM, (3 * tok, wide), bf16)] * len(part),
                12 * tok * model_width,
                8 * tok * model_width,
            )(assign, q, k, v, q_gain[None], k_gain[None], steps)
        fresh = exchange(bundles, order)
        gate = lax.dynamic_slice(gate_table, (timestep[0], device % slots * wide), (1, wide))
        state = []

        def step(s, outs, extra):
            given = [*fresh, stale[s - 1], *state, *extra]
            return call(
                functools.partial(
                    attend_kernel, order, tok, blocks, heads, rows in rare, s, len(state)
                ),
                "attend",
                [SMEM] * 2 + [VMEM] * len(given),
                outs,
                8 * block_rows * block_rows * wide,
                16 * block_rows * wide,
            )(assign, counts, *given)

        for s in range(1, blocks - 1):
            state = step(s, [(VMEM, (block_rows, n), f32) for n in (HEAD, wide)], [])
        outs = step(blocks - 1, [(VMEM, (tok, wide), bf16)] * slots, [gate])
        back_order = [3, 1, 6, 7, 4, 5, 2, 0] if rows == sizes[0] else [6, 7, 4, 5, 2, 3, 1, 0]
        back = exchange([outs[order.index(d)] for d in back_order], back_order)
        new_keys, new_values = call(
            functools.partial(cache_kernel, order, tok),
            "cache",
            [VMEM] * slots,
            [(VMEM, (1, block_rows, wide), bf16)] * 2,
            0,
            8 * block_rows * wide,
        )(*fresh)
        (mixed,) = call(
            functools.partial(collect_kernel, back_order, heads),
            "collect",
            [VMEM] * len(back),
            [(VMEM, (tok, model_width), bf16)],
            0,
            4 * tok * model_width,
        )(*back)
        return mixed, new_keys, new_values

    operands = (
        assign,
        counts,
        stale_keys,
        stale_values,
        q_fresh,
        k_fresh,
        v_fresh,
        q_gain,
        k_gain,
        gate_table,
        timestep,
    )
    return lax.switch(which[0], [functools.partial(run, rows) for rows in sizes], operands)


def solution(mesh):
    rows = P(("groups", "seq"), None)
    entries = P(("groups", "seq"), None, None)
    return jax.shard_map(
        body,
        mesh=mesh,
        in_specs=(
            rows,
            rows,
            rows,
            P(),
            P(),
            entries,
            entries,
            P(),
            P("groups"),
            P("groups"),
            P("groups"),
        ),
        out_specs=(rows, entries, entries),
        check_vma=False,
    )
```

profile of v0, /device:TPU:0, one launch (start us, length us, event | category | flops | bytes accessed | tf_op | source)
XLA Modules:
  0.0 73.2 jit_solution(10863520841443316142)
XLA Ops:
  0.6 1.2 %choose.1 = s32[1]{0:T(128)} custom-call(s32[16]{0:T(128)} %assign.1, s32[16]{0:T(128)} %counts.1), custom_call_target="tpu_custom_call" | custom-call | bytes 5242880 | tf_op jit(solution)/shard_map/choose/pallas_call | solution.py:259
  2.5 69.9 %conditional.1 = (bf16[1,512,640]{2,1,0:T(8,128)(2,1)}, bf16[1,512,640]{2,1,0:T(8,128)(2,1)}, bf16[64,5120]{1,0:T(8,128)(2,1)S(1)}) conditional(s32[]{:T(128)} %bitcast.3, (bf16[5120]{0:T(1024)(128)(2,1)}, bf16[5120]{0:T(1024)(128)(2,1)}, s32[16]{0:T(128)}, bf16[64,5120]{1,0:T(8,128)(2,1)}, bf16[64,5120]{1,0:T(8,128)(2,1)}, ...), branch_computations={%region_0.1_spmd, %region_1.2_spmd, %region_2.3_spmd} | conditional | flops 2021130240 | bytes 39450632 | solution.py:348
  2.6 2.3 %compact.3 = bf16[416,1280]{1,0:T(8,128)(2,1)S(1)} custom-call(s32[16]{0:T(128)} %get-tuple-element.78.assign, s32[16]{0:T(128)} %get-tuple-element.79.counts, bf16[1,512,640]{2,1,0:T(8,128)(2,1)} %get-tuple-element.94.keys, bf16[1,512,640]{2,1,0:T(8,128)(2,1)} %get-tuple-element.95.values), custom_call_target="tpu_custom_call" | custom-call | flops 545259520 | bytes 2375680 | tf_op jit(solution)/shard_map/cond/branch_0_fun/compact/pallas_call | solution.py:276
  4.9 4.1 %collective-permute-start.7 = (bf16[416,1280]{1,0:T(8,128)(2,1)S(1)}, bf16[416,1280]{1,0:T(8,128)(2,1)}, u32[]{:S(2)}, u32[]{:S(2)}) collective-permute-start(bf16[416,1280]{1,0:T(8,128)(2,1)S(1)} %compact.3), channel_id=1, source_target_pairs={{0,8},{1,9},{2,10},{3,11},{4,12},{5,13},{6,14},{7,15},{8,0},{9,1},... | collective-permute-start | bytes 3194888 | tf_op jit(solution)/shard_map/cond/branch_0_fun/ppermute | solution.py:39
  9.1 1.7 %norm.6 = (bf16[192,640]{1,0:T(8,128)(2,1)S(1)}, bf16[192,640]{1,0:T(8,128)(2,1)S(1)}, bf16[192,640]{1,0:T(8,128)(2,1)S(1)}, bf16[192,640]{1,0:T(8,128)(2,1)S(1)}) custom-call(s32[16]{0:T(128)S(1)} %copy-done.16, bf16[64,5120]{1,0:T(8,128)(2,1)S(1)} %copy-done, bf16[64,5120]{1,0:T(8,128)(2,1)S(1)} %copy-done.3, bf16[64,5120]{1,0:T(8,128)(2,1)S(1)} %copy-done.6, ...), custom_call_target="tpu_custom_call" | custom-call | flops 3932160 | bytes 2621440 | tf_op jit(solution)/shard_map/cond/branch_0_fun/norm/pallas_call | solution.py:287
  10.8 2.6 %collective-permute-start = (bf16[192,640]{1,0:T(8,128)(2,1)S(1)}, bf16[192,640]{1,0:T(8,128)(2,1)S(1)}, u32[]{:S(2)}, u32[]{:S(2)}) collective-permute-start(bf16[192,640]{1,0:T(8,128)(2,1)S(1)} %get-tuple-element.86), channel_id=1, source_target_pairs={{0,6},{1,7},{2,4},{3,5},{4,2},{5,3},{6,0},{7,1},{8,14},{9,15},{10,... | collective-permute-start | bytes 737288 | tf_op jit(solution)/shard_map/cond/branch_0_fun/ppermute | solution.py:35
  13.3 0.4 collective-permute-start.1
  13.8 0.1 collective-permute-start.2
  13.9 1.6 %collective-permute-start.3 = (bf16[192,640]{1,0:T(8,128)(2,1)S(1)}, bf16[192,640]{1,0:T(8,128)(2,1)S(1)}, u32[]{:S(2)}, u32[]{:S(2)}) collective-permute-start(bf16[192,640]{1,0:T(8,128)(2,1)S(1)} %get-tuple-element.89), channel_id=1, source_target_pairs={{0,5},{1,4},{2,7},{3,6},{4,1},{5,0},{6,3},{7,2},{8,13},{9,12},{10,... | collective-permute-start | bytes 737288 | tf_op jit(solution)/shard_map/cond/branch_0_fun/ppermute | solution.py:35
  15.5 2.4 %norm.7 = (bf16[192,640]{1,0:T(8,128)(2,1)}, bf16[192,640]{1,0:T(8,128)(2,1)}, bf16[192,640]{1,0:T(8,128)(2,1)S(1)}, bf16[192,640]{1,0:T(8,128)(2,1)S(1)}) custom-call(s32[16]{0:T(128)S(1)} %copy-done.16, bf16[64,5120]{1,0:T(8,128)(2,1)S(1)} %copy-done, bf16[64,5120]{1,0:T(8,128)(2,1)S(1)} %copy-done.3, bf16[64,5120]{1,0:T(8,128)(2,1)S(1)} %copy-done.6, ...), custom_call_target="tpu_custom_call" | custom-call | flops 3932160 | bytes 2621440 | tf_op jit(solution)/shard_map/cond/branch_0_fun/norm/pallas_call | solution.py:287
  18.0 20.2 %collective-permute-done.refs_0_ = bf16[192,640]{1,0:T(8,128)(2,1)S(1)} collective-permute-done((bf16[192,640]{1,0:T(8,128)(2,1)S(1)}, bf16[192,640]{1,0:T(8,128)(2,1)S(1)}, u32[]{:S(2)}, u32[]{:S(2)}) %collective-permute-start) | collective-permute-done | bytes 245792 | tf_op jit(solution)/shard_map/cond/branch_0_fun/ppermute | solution.py:35
  38.2 1.5 %collective-permute-start.4 = (bf16[192,640]{1,0:T(8,128)(2,1)}, bf16[192,640]{1,0:T(8,128)(2,1)S(1)}, u32[]{:S(2)}, u32[]{:S(2)}) collective-permute-start(bf16[192,640]{1,0:T(8,128)(2,1)} %get-tuple-element.90), channel_id=1, source_target_pairs={{0,2},{1,3},{2,0},{3,1},{4,6},{5,7},{6,4},{7,5},{8,10},{9,11},{10,... | collective-permute-start | bytes 737288 | tf_op jit(solution)/shard_map/cond/branch_0_fun/ppermute | solution.py:35
  39.7 3.8 %collective-permute-done.1.refs_1_ = bf16[192,640]{1,0:T(8,128)(2,1)S(1)} collective-permute-done((bf16[192,640]{1,0:T(8,128)(2,1)S(1)}, bf16[192,640]{1,0:T(8,128)(2,1)S(1)}, u32[]{:S(2)}, u32[]{:S(2)}) %collective-permute-start.1) | collective-permute-done | bytes 245792 | tf_op jit(solution)/shard_map/cond/branch_0_fun/ppermute | solution.py:35
  43.5 5.3 %collective-permute-done.2.refs_2_ = bf16[192,640]{1,0:T(8,128)(2,1)S(1)} collective-permute-done((bf16[192,640]{1,0:T(8,128)(2,1)S(1)}, bf16[192,640]{1,0:T(8,128)(2,1)S(1)}, u32[]{:S(2)}, u32[]{:S(2)}) %collective-permute-start.2) | collective-permute-done | bytes 245792 | tf_op jit(solution)/shard_map/cond/branch_0_fun/ppermute | solution.py:35
  50.7 0.8 %dynamic_slice.6.refs_9_ = bf16[1,640]{1,0:T(2,128)(2,1)S(1)} dynamic-slice(bf16[50,5120]{1,0:T(8,128)(2,1)} %get-tuple-element.96, s32[]{:T(128)S(6)} %select_n.24, s32[]{:T(128)S(6)} %select_n.26), dynamic_slice_sizes={1,640} | dynamic-slice | bytes 2564 | tf_op jit(solution)/shard_map/cond/branch_0_fun/dynamic_slice | solution.py:296
  51.5 1.4 %collective-permute-done.3.refs_3_ = bf16[192,640]{1,0:T(8,128)(2,1)S(1)} collective-permute-done((bf16[192,640]{1,0:T(8,128)(2,1)S(1)}, bf16[192,640]{1,0:T(8,128)(2,1)S(1)}, u32[]{:S(2)}, u32[]{:S(2)}) %collective-permute-start.3) | collective-permute-done | bytes 245792 | tf_op jit(solution)/shard_map/cond/branch_0_fun/ppermute | solution.py:35
  52.9 2.6 %collective-permute-done.7.refs_8_ = bf16[416,1280]{1,0:T(8,128)(2,1)} collective-permute-done((bf16[416,1280]{1,0:T(8,128)(2,1)S(1)}, bf16[416,1280]{1,0:T(8,128)(2,1)}, u32[]{:S(2)}, u32[]{:S(2)}) %collective-permute-start.7) | collective-permute-done | bytes 1064992 | tf_op jit(solution)/shard_map/cond/branch_0_fun/ppermute | solution.py:39
  55.5 5.2 %attend.3 = (bf16[64,640]{1,0:T(8,128)(2,1)S(1)}, bf16[64,640]{1,0:T(8,128)(2,1)S(1)}, bf16[64,640]{1,0:T(8,128)(2,1)S(1)}, bf16[64,640]{1,0:T(8,128)(2,1)S(1)},...) custom-call(s32[16]{0:T(128)S(1)} %copy-done.16, ...), custom_call_target="tpu_custom_call" | custom-call | flops 1342177280 | bytes 5242880 | tf_op jit(solution)/shard_map/cond/branch_0_fun/attend/pallas_call | solution.py:301
  60.8 1.8 %collective-permute-start.10 = (bf16[64,640]{1,0:T(8,128)(2,1)S(1)}, bf16[64,640]{1,0:T(8,128)(2,1)S(1)}, u32[]{:S(2)}, u32[]{:S(2)}) collective-permute-start(bf16[64,640]{1,0:T(8,128)(2,1)S(1)} %get-tuple-element.101), channel_id=1, source_target_pairs={{0,6},{1,7},{2,4},{3,5},{4,2},{5,3},{6,0},{7,1},{8,14},{9,15},{10,... | collective-permute-start | bytes 245768 | tf_op jit(solution)/shard_map/cond/branch_0_fun/ppermute | solution.py:35
  62.6 1.5 %collective-permute-start.11 = (bf16[64,640]{1,0:T(8,128)(2,1)S(1)}, bf16[64,640]{1,0:T(8,128)(2,1)S(1)}, u32[]{:S(2)}, u32[]{:S(2)}) collective-permute-start(bf16[64,640]{1,0:T(8,128)(2,1)S(1)} %get-tuple-element.102), channel_id=1, source_target_pairs={{0,7},{1,6},{2,5},{3,4},{4,3},{5,2},{6,1},{7,0},{8,15},{9,14},{10,... | collective-permute-start | bytes 245768 | tf_op jit(solution)/shard_map/cond/branch_0_fun/ppermute | solution.py:35
  64.1 1.5 %collective-permute-start.12 = (bf16[64,640]{1,0:T(8,128)(2,1)S(1)}, bf16[64,640]{1,0:T(8,128)(2,1)S(1)}, u32[]{:S(2)}, u32[]{:S(2)}) collective-permute-start(bf16[64,640]{1,0:T(8,128)(2,1)S(1)} %get-tuple-element.103), channel_id=1, source_target_pairs={{0,4},{1,5},{2,6},{3,7},{4,0},{5,1},{6,2},{7,3},{8,12},{9,13},{10,... | collective-permute-start | bytes 245768 | tf_op jit(solution)/shard_map/cond/branch_0_fun/ppermute | solution.py:35
  65.5 1.2 %collective-permute-start.14 = (bf16[64,640]{1,0:T(8,128)(2,1)S(1)}, bf16[64,640]{1,0:T(8,128)(2,1)S(1)}, u32[]{:S(2)}, u32[]{:S(2)}) collective-permute-start(bf16[64,640]{1,0:T(8,128)(2,1)S(1)} %get-tuple-element.105), channel_id=1, source_target_pairs={{0,2},{1,3},{2,0},{3,1},{4,6},{5,7},{6,4},{7,5},{8,10},{9,11},{10,... | collective-permute-start | bytes 245768 | tf_op jit(solution)/shard_map/cond/branch_0_fun/ppermute | solution.py:35
  66.8 0.2 collective-permute-done.10.refs_2_
  67.0 0.6 collective-permute-start.8
  67.6 1.1 %collective-permute-done.11.refs_3_ = bf16[64,640]{1,0:T(8,128)(2,1)S(1)} collective-permute-done((bf16[64,640]{1,0:T(8,128)(2,1)S(1)}, bf16[64,640]{1,0:T(8,128)(2,1)S(1)}, u32[]{:S(2)}, u32[]{:S(2)}) %collective-permute-start.11) | collective-permute-done | bytes 81952 | tf_op jit(solution)/shard_map/cond/branch_0_fun/ppermute | solution.py:35
  68.7 0.1 collective-permute-start.9
  68.8 1.2 %cache.3 = (bf16[1,512,640]{2,1,0:T(8,128)(2,1)}, bf16[1,512,640]{2,1,0:T(8,128)(2,1)}) custom-call(bf16[192,640]{1,0:T(8,128)(2,1)S(1)} %collective-permute-done.refs_0_, bf16[192,640]{1,0:T(8,128)(2,1)S(1)} %collective-permute-done.1.refs_1_, bf16[192,640]{1,0:T(8,128)(2,1)S(1)} %collective-permute-done.2.refs_2_, ...), custom_call_target="tpu_custom_call" | custom-call | bytes 2621440 | tf_op jit(solution)/shard_map/cond/branch_0_fun/cache/pallas_call | solution.py:317
  70.0 0.6 collective-permute-done.12.refs_4_
  70.6 0.2 collective-permute-done.14.refs_6_
  70.9 1.2 %collective-permute-done.8.refs_0_ = bf16[64,640]{1,0:T(8,128)(2,1)S(1)} collective-permute-done((bf16[64,640]{1,0:T(8,128)(2,1)S(1)}, bf16[64,640]{1,0:T(8,128)(2,1)S(1)}, u32[]{:S(2)}, u32[]{:S(2)}) %collective-permute-start.8) | collective-permute-done | bytes 81952 | tf_op jit(solution)/shard_map/cond/branch_0_fun/ppermute | solution.py:35
  72.1 0.1 collect.3
  72.4 0.8 %copy-done.9 = bf16[64,5120]{1,0:T(8,128)(2,1)} copy-done((bf16[64,5120]{1,0:T(8,128)(2,1)}, bf16[64,5120]{1,0:T(8,128)(2,1)S(1)}, u32[]{:S(2)}) %copy-start.9) | copy-done | bytes 655384
  (27 shorter events, 0.1 us)
Async XLA Ops:
  2.5 6.5 %copy-start.10 = (bf16[5120]{0:T(1024)(128)(2,1)S(1)}, bf16[5120]{0:T(1024)(128)(2,1)}, u32[]{:S(2)}) copy-start(bf16[5120]{0:T(1024)(128)(2,1)} %get-tuple-element.83) | copy-start | bytes 30724 | tf_op jit(solution)/shard_map/cond
  2.5 6.5 %copy-start.13 = (bf16[5120]{0:T(1024)(128)(2,1)S(1)}, bf16[5120]{0:T(1024)(128)(2,1)}, u32[]{:S(2)}) copy-start(bf16[5120]{0:T(1024)(128)(2,1)} %get-tuple-element.84) | copy-start | bytes 30724 | tf_op jit(solution)/shard_map/cond
  2.5 6.5 %copy-start = (bf16[64,5120]{1,0:T(8,128)(2,1)S(1)}, bf16[64,5120]{1,0:T(8,128)(2,1)}, u32[]{:S(2)}) copy-start(bf16[64,5120]{1,0:T(8,128)(2,1)} %get-tuple-element.80.q) | copy-start | bytes 1966084 | tf_op jit(solution)/shard_map/cond
  2.6 6.5 %copy-start.3 = (bf16[64,5120]{1,0:T(8,128)(2,1)S(1)}, bf16[64,5120]{1,0:T(8,128)(2,1)}, u32[]{:S(2)}) copy-start(bf16[64,5120]{1,0:T(8,128)(2,1)} %get-tuple-element.81.k) | copy-start | bytes 1966084 | tf_op jit(solution)/shard_map/cond
  2.6 6.5 %copy-start.6 = (bf16[64,5120]{1,0:T(8,128)(2,1)S(1)}, bf16[64,5120]{1,0:T(8,128)(2,1)}, u32[]{:S(2)}) copy-start(bf16[64,5120]{1,0:T(8,128)(2,1)} %get-tuple-element.82.v) | copy-start | bytes 1966084 | tf_op jit(solution)/shard_map/cond
  2.6 6.5 %copy-start.16 = (s32[16]{0:T(128)S(1)}, s32[16]{0:T(128)}, u32[]{:S(2)}) copy-start(s32[16]{0:T(128)} %get-tuple-element.78.assign) | copy-start | bytes 196 | tf_op jit(solution)/shard_map/cond
  2.6 6.5 %copy-start.19 = (f32[1,128]{1,0:T(1,128)S(1)}, f32[1,128]{1,0:T(1,128)}, u32[]{:S(2)}) copy-start(f32[1,128]{1,0:T(1,128)} %get-tuple-element.85.steps) | copy-start | bytes 1540 | tf_op jit(solution)/shard_map/cond
  4.9 50.6 %collective-permute-start.7 = (bf16[416,1280]{1,0:T(8,128)(2,1)S(1)}, bf16[416,1280]{1,0:T(8,128)(2,1)}, u32[]{:S(2)}, u32[]{:S(2)}) collective-permute-start(bf16[416,1280]{1,0:T(8,128)(2,1)S(1)} %compact.3), channel_id=1, source_target_pairs={{0,8},{1,9},{2,10},{3,11},{4,12},{5,13},{6,14},{7,15},{8,0},{9,1},... | collective-permute-start | bytes 3194888 | tf_op jit(solution)/shard_map/cond/branch_0_fun/ppermute | solution.py:39
  10.8 44.8 %copy-start.22 = (s32[16]{0:T(128)S(1)}, s32[16]{0:T(128)}, u32[]{:S(2)}) copy-start(s32[16]{0:T(128)} %get-tuple-element.79.counts) | copy-start | bytes 196 | tf_op jit(solution)/shard_map/cond
  10.8 27.4 %collective-permute-start = (bf16[192,640]{1,0:T(8,128)(2,1)S(1)}, bf16[192,640]{1,0:T(8,128)(2,1)S(1)}, u32[]{:S(2)}, u32[]{:S(2)}) collective-permute-start(bf16[192,640]{1,0:T(8,128)(2,1)S(1)} %get-tuple-element.86), channel_id=1, source_target_pairs={{0,6},{1,7},{2,4},{3,5},{4,2},{5,3},{6,0},{7,1},{8,14},{9,15},{10,... | collective-permute-start | bytes 737288 | tf_op jit(solution)/shard_map/cond/branch_0_fun/ppermute | solution.py:35
  13.3 30.1 %collective-permute-start.1 = (bf16[192,640]{1,0:T(8,128)(2,1)S(1)}, bf16[192,640]{1,0:T(8,128)(2,1)S(1)}, u32[]{:S(2)}, u32[]{:S(2)}) collective-permute-start(bf16[192,640]{1,0:T(8,128)(2,1)S(1)} %get-tuple-element.87), channel_id=1, source_target_pairs={{0,4},{1,5},{2,6},{3,7},{4,0},{5,1},{6,2},{7,3},{8,12},{9,13},{10,... | collective-permute-start | bytes 737288 | tf_op jit(solution)/shard_map/cond/branch_0_fun/ppermute | solution.py:35
  13.8 35.0 %collective-permute-start.2 = (bf16[192,640]{1,0:T(8,128)(2,1)S(1)}, bf16[192,640]{1,0:T(8,128)(2,1)S(1)}, u32[]{:S(2)}, u32[]{:S(2)}) collective-permute-start(bf16[192,640]{1,0:T(8,128)(2,1)S(1)} %get-tuple-element.88), channel_id=1, source_target_pairs={{0,7},{1,6},{2,5},{3,4},{4,3},{5,2},{6,1},{7,0},{8,15},{9,14},{10,... | collective-permute-start | bytes 737288 | tf_op jit(solution)/shard_map/cond/branch_0_fun/ppermute | solution.py:35
  13.9 38.9 %collective-permute-start.3 = (bf16[192,640]{1,0:T(8,128)(2,1)S(1)}, bf16[192,640]{1,0:T(8,128)(2,1)S(1)}, u32[]{:S(2)}, u32[]{:S(2)}) collective-permute-start(bf16[192,640]{1,0:T(8,128)(2,1)S(1)} %get-tuple-element.89), channel_id=1, source_target_pairs={{0,5},{1,4},{2,7},{3,6},{4,1},{5,0},{6,3},{7,2},{8,13},{9,12},{10,... | collective-permute-start | bytes 737288 | tf_op jit(solution)/shard_map/cond/branch_0_fun/ppermute | solution.py:35
  38.2 14.7 %collective-permute-start.4 = (bf16[192,640]{1,0:T(8,128)(2,1)}, bf16[192,640]{1,0:T(8,128)(2,1)S(1)}, u32[]{:S(2)}, u32[]{:S(2)}) collective-permute-start(bf16[192,640]{1,0:T(8,128)(2,1)} %get-tuple-element.90), channel_id=1, source_target_pairs={{0,2},{1,3},{2,0},{3,1},{4,6},{5,7},{6,4},{7,5},{8,10},{9,11},{10,... | collective-permute-start | bytes 737288 | tf_op jit(solution)/shard_map/cond/branch_0_fun/ppermute | solution.py:35
  43.5 9.4 %collective-permute-start.5 = (bf16[192,640]{1,0:T(8,128)(2,1)}, bf16[192,640]{1,0:T(8,128)(2,1)S(1)}, u32[]{:S(2)}, u32[]{:S(2)}) collective-permute-start(bf16[192,640]{1,0:T(8,128)(2,1)} %get-tuple-element.91), channel_id=1, source_target_pairs={{0,3},{1,2},{2,1},{3,0},{4,7},{5,6},{6,5},{7,4},{8,11},{9,10},{10,... | collective-permute-start | bytes 737288 | tf_op jit(solution)/shard_map/cond/branch_0_fun/ppermute | solution.py:35
  48.8 4.1 %collective-permute-start.6 = (bf16[192,640]{1,0:T(8,128)(2,1)S(1)}, bf16[192,640]{1,0:T(8,128)(2,1)S(1)}, u32[]{:S(2)}, u32[]{:S(2)}) collective-permute-start(bf16[192,640]{1,0:T(8,128)(2,1)S(1)} %get-tuple-element.92), channel_id=1, source_target_pairs={{0,1},{1,0},{2,3},{3,2},{4,5},{5,4},{6,7},{7,6},{8,9},{9,8},{10,11... | collective-permute-start | bytes 737288 | tf_op jit(solution)/shard_map/cond/branch_0_fun/ppermute | solution.py:35
  60.8 6.3 %collective-permute-start.10 = (bf16[64,640]{1,0:T(8,128)(2,1)S(1)}, bf16[64,640]{1,0:T(8,128)(2,1)S(1)}, u32[]{:S(2)}, u32[]{:S(2)}) collective-permute-start(bf16[64,640]{1,0:T(8,128)(2,1)S(1)} %get-tuple-element.101), channel_id=1, source_target_pairs={{0,6},{1,7},{2,4},{3,5},{4,2},{5,3},{6,0},{7,1},{8,14},{9,15},{10,... | collective-permute-start | bytes 245768 | tf_op jit(solution)/shard_map/cond/branch_0_fun/ppermute | solution.py:35
  62.6 6.1 %collective-permute-start.11 = (bf16[64,640]{1,0:T(8,128)(2,1)S(1)}, bf16[64,640]{1,0:T(8,128)(2,1)S(1)}, u32[]{:S(2)}, u32[]{:S(2)}) collective-permute-start(bf16[64,640]{1,0:T(8,128)(2,1)S(1)} %get-tuple-element.102), channel_id=1, source_target_pairs={{0,7},{1,6},{2,5},{3,4},{4,3},{5,2},{6,1},{7,0},{8,15},{9,14},{10,... | collective-permute-start | bytes 245768 | tf_op jit(solution)/shard_map/cond/branch_0_fun/ppermute | solution.py:35
  64.1 6.6 %collective-permute-start.12 = (bf16[64,640]{1,0:T(8,128)(2,1)S(1)}, bf16[64,640]{1,0:T(8,128)(2,1)S(1)}, u32[]{:S(2)}, u32[]{:S(2)}) collective-permute-start(bf16[64,640]{1,0:T(8,128)(2,1)S(1)} %get-tuple-element.103), channel_id=1, source_target_pairs={{0,4},{1,5},{2,6},{3,7},{4,0},{5,1},{6,2},{7,3},{8,12},{9,13},{10,... | collective-permute-start | bytes 245768 | tf_op jit(solution)/shard_map/cond/branch_0_fun/ppermute | solution.py:35
  65.5 5.1 %collective-permute-start.13 = (bf16[64,640]{1,0:T(8,128)(2,1)S(1)}, bf16[64,640]{1,0:T(8,128)(2,1)S(1)}, u32[]{:S(2)}, u32[]{:S(2)}) collective-permute-start(bf16[64,640]{1,0:T(8,128)(2,1)S(1)} %get-tuple-element.104), channel_id=1, source_target_pairs={{0,5},{1,4},{2,7},{3,6},{4,1},{5,0},{6,3},{7,2},{8,13},{9,12},{10,... | collective-permute-start | bytes 245768 | tf_op jit(solution)/shard_map/cond/branch_0_fun/ppermute | solution.py:35
  65.5 5.3 %collective-permute-start.14 = (bf16[64,640]{1,0:T(8,128)(2,1)S(1)}, bf16[64,640]{1,0:T(8,128)(2,1)S(1)}, u32[]{:S(2)}, u32[]{:S(2)}) collective-permute-start(bf16[64,640]{1,0:T(8,128)(2,1)S(1)} %get-tuple-element.105), channel_id=1, source_target_pairs={{0,2},{1,3},{2,0},{3,1},{4,6},{5,7},{6,4},{7,5},{8,10},{9,11},{10,... | collective-permute-start | bytes 245768 | tf_op jit(solution)/shard_map/cond/branch_0_fun/ppermute | solution.py:35
  67.0 5.1 %collective-permute-start.8 = (bf16[64,640]{1,0:T(8,128)(2,1)S(1)}, bf16[64,640]{1,0:T(8,128)(2,1)S(1)}, u32[]{:S(2)}, u32[]{:S(2)}) collective-permute-start(bf16[64,640]{1,0:T(8,128)(2,1)S(1)} %get-tuple-element.99), channel_id=1, source_target_pairs={{0,3},{1,2},{2,1},{3,0},{4,7},{5,6},{6,5},{7,4},{8,11},{9,10},{10,... | collective-permute-start | bytes 245768 | tf_op jit(solution)/shard_map/cond/branch_0_fun/ppermute | solution.py:35
  68.7 3.4 %collective-permute-start.9 = (bf16[64,640]{1,0:T(8,128)(2,1)S(1)}, bf16[64,640]{1,0:T(8,128)(2,1)S(1)}, u32[]{:S(2)}, u32[]{:S(2)}) collective-permute-start(bf16[64,640]{1,0:T(8,128)(2,1)S(1)} %get-tuple-element.100), channel_id=1, source_target_pairs={{0,1},{1,0},{2,3},{3,2},{4,5},{5,4},{6,7},{7,6},{8,9},{9,8},{10,11... | collective-permute-start | bytes 245768 | tf_op jit(solution)/shard_map/cond/branch_0_fun/ppermute | solution.py:35
  72.4 0.8 %copy-start.9 = (bf16[64,5120]{1,0:T(8,128)(2,1)}, bf16[64,5120]{1,0:T(8,128)(2,1)S(1)}, u32[]{:S(2)}) copy-start(bf16[64,5120]{1,0:T(8,128)(2,1)S(1)} %get-tuple-element.174) | copy-start | bytes 1966084
where the time goes:
time: 73.5 us; the launch traced here: 73.2 us
  waiting for transfers between devices  36.8 us (50%)
  starting transfers between devices  17 us (23%)
  Pallas kernels  14.1 us (19%)
  loops' own time  2.35 us (3%)
  local copies, waits for them, and re-layouts  1.7 us (2%)
  between operations  1.31 us (2%)
    ppermute x14, waiting for transfers between devices, to_partner(): return lax.ppermute(value, 'seq', [(i, i ^ distance) for i in range(size)])  34.2 us
    ppermute x14, starting transfers between devices, to_partner(): return lax.ppermute(value, 'seq', [(i, i ^ distance) for i in range(size)])  12.9 us
    pallas_call x1, Pallas kernels, step(): call(functools.partial(attend_kernel, order, tok, blocks, heads, rows in...  5.24 us
    pallas_call x2, Pallas kernels, run(): call(functools.partial(norm_kernel, slots, part, heads), 'norm', [SMEM] +...  4.14 us
    ppermute x1, starting transfers between devices, to_block(): lax.ppermute(value, 'seq', [(i, (i + distance) % size) for i in range(siz...  4.1 us
    ppermute x1, waiting for transfers between devices, to_block(): lax.ppermute(value, 'seq', [(i, (i + distance) % size) for i in range(siz...  2.61 us
    another operation x1, loops' own time, body(): lax.switch(which[0], [functools.partial(run, rows) for rows in sizes], op...  2.35 us
    pallas_call x1, Pallas kernels, run(): call(functools.partial(compact_kernel, slots, tok), 'compact', [SMEM] * 2...  2.25 us
  transfers between devices with their start and end apart: 15, of which 10 were waited for; matrix products, arithmetic and copies ran while one was open for 1% of the time, Pallas kernels for 7%

commit v1 on v0

--- a/solution.py
+++ b/solution.py
@@ -253,7 +253,7 @@
     blocks = size // slots
     heads = wide // HEAD
     order = [6, 4, 7, 5, 2, 3, 1, 0]
-    sizes = [block_rows * n // 32 for n in (26, 28, 32)] if blocks == 2 else [block_rows]
+    sizes = [block_rows * n // 32 for n in (27, 28, 32)] if blocks == 2 else [block_rows]
     rare = sizes[2:]
 
     (which,) = call(

time: 73.5 us -> 74.4 us (1.012)
  waiting for transfers between devices: 36.8 us -> 37.6 us
    ppermute x1, waiting for transfers between devices: 2.61 us -> 3.49 us  [to_block(): lax.ppermute(value, 'seq', [(i, (i + distance) % size) for i in range(siz...]
  transfers between devices with their start and end apart: 15 -> 15, of which waited for: 10 -> 8; matrix products, arithmetic and copies ran while one was open for 1% -> 1% of each run, Pallas kernels for 7% -> 7%
where the time goes in v1:
time: 74.4 us; the launch traced here: 74.2 us
  waiting for transfers between devices  37.6 us (51%)
  starting transfers between devices  17 us (23%)
  Pallas kernels  14.2 us (19%)
  loops' own time  2.35 us (3%)
  local copies, waits for them, and re-layouts  1.7 us (2%)
  between operations  1.31 us (2%)
    ppermute x14, waiting for transfers between devices, to_partner(): return lax.ppermute(value, 'seq', [(i, i ^ distance) for i in range(size)])  34.1 us
    ppermute x14, starting transfers between devices, to_partner(): return lax.ppermute(value, 'seq', [(i, i ^ distance) for i in range(size)])  12.9 us
    pallas_call x1, Pallas kernels, step(): call(functools.partial(attend_kernel, order, tok, blocks, heads, rows in...  5.26 us
    pallas_call x2, Pallas kernels, run(): call(functools.partial(norm_kernel, slots, part, heads), 'norm', [SMEM] +...  4.2 us
    ppermute x1, starting transfers between devices, to_block(): lax.ppermute(value, 'seq', [(i, (i + distance) % size) for i in range(siz...  4.1 us
    ppermute x1, waiting for transfers between devices, to_block(): lax.ppermute(value, 'seq', [(i, (i + distance) % size) for i in range(siz...  3.49 us
    another operation x1, loops' own time, body(): lax.switch(which[0], [functools.partial(run, rows) for rows in sizes], op...  2.35 us
    pallas_call x1, Pallas kernels, run(): call(functools.partial(compact_kernel, slots, tok), 'compact', [SMEM] * 2...  2.28 us
  transfers between devices with their start and end apart: 15, of which 8 were waited for; matrix products, arithmetic and copies ran while one was open for 1% of the time, Pallas kernels for 7%

profile of v1, /device:TPU:0, one launch (start us, length us, event | category | flops | bytes accessed | tf_op | source)
XLA Modules:
  0.0 74.2 jit_solution(16132026034227538748)
XLA Ops:
  0.6 1.2 %choose.1 = s32[1]{0:T(128)} custom-call(s32[16]{0:T(128)} %assign.1, s32[16]{0:T(128)} %counts.1), custom_call_target="tpu_custom_call" | custom-call | bytes 5242880 | tf_op jit(solution)/shard_map/choose/pallas_call | solution.py:259
  2.5 70.8 %conditional.1 = (bf16[1,512,640]{2,1,0:T(8,128)(2,1)}, bf16[1,512,640]{2,1,0:T(8,128)(2,1)}, bf16[64,5120]{1,0:T(8,128)(2,1)S(1)}) conditional(s32[]{:T(128)} %bitcast.3, (bf16[5120]{0:T(1024)(128)(2,1)}, bf16[5120]{0:T(1024)(128)(2,1)}, s32[16]{0:T(128)}, bf16[64,5120]{1,0:T(8,128)(2,1)}, bf16[64,5120]{1,0:T(8,128)(2,1)}, ...), branch_computations={%region_0.1_spmd, %region_1.2_spmd, %region_2.3_spmd} | conditional | flops 2021130240 | bytes 39450632 | solution.py:348
  2.6 0.0 copy-start.19
  2.6 2.3 %compact.3 = bf16[432,1280]{1,0:T(8,128)(2,1)S(1)} custom-call(s32[16]{0:T(128)} %get-tuple-element.78.assign, s32[16]{0:T(128)} %get-tuple-element.79.counts, bf16[1,512,640]{2,1,0:T(8,128)(2,1)} %get-tuple-element.94.keys, bf16[1,512,640]{2,1,0:T(8,128)(2,1)} %get-tuple-element.95.values), custom_call_target="tpu_custom_call" | custom-call | flops 566231040 | bytes 2416640 | tf_op jit(solution)/shard_map/cond/branch_0_fun/compact/pallas_call | solution.py:276
  4.9 4.1 %collective-permute-start.7 = (bf16[432,1280]{1,0:T(8,128)(2,1)S(1)}, bf16[432,1280]{1,0:T(8,128)(2,1)}, u32[]{:S(2)}, u32[]{:S(2)}) collective-permute-start(bf16[432,1280]{1,0:T(8,128)(2,1)S(1)} %compact.3), channel_id=1, source_target_pairs={{0,8},{1,9},{2,10},{3,11},{4,12},{5,13},{6,14},{7,15},{8,0},{9,1},... | collective-permute-start | bytes 3317768 | tf_op jit(solution)/shard_map/cond/branch_0_fun/ppermute | solution.py:39
  9.1 1.7 %norm.6 = (bf16[192,640]{1,0:T(8,128)(2,1)S(1)}, bf16[192,640]{1,0:T(8,128)(2,1)S(1)}, bf16[192,640]{1,0:T(8,128)(2,1)S(1)}, bf16[192,640]{1,0:T(8,128)(2,1)S(1)}) custom-call(s32[16]{0:T(128)S(1)} %copy-done.16, bf16[64,5120]{1,0:T(8,128)(2,1)S(1)} %copy-done, bf16[64,5120]{1,0:T(8,128)(2,1)S(1)} %copy-done.3, bf16[64,5120]{1,0:T(8,128)(2,1)S(1)} %copy-done.6, ...), custom_call_target="tpu_custom_call" | custom-call | flops 3932160 | bytes 2621440 | tf_op jit(solution)/shard_map/cond/branch_0_fun/norm/pallas_call | solution.py:287
  10.8 2.6 %collective-permute-start = (bf16[192,640]{1,0:T(8,128)(2,1)S(1)}, bf16[192,640]{1,0:T(8,128)(2,1)S(1)}, u32[]{:S(2)}, u32[]{:S(2)}) collective-permute-start(bf16[192,640]{1,0:T(8,128)(2,1)S(1)} %get-tuple-element.86), channel_id=1, source_target_pairs={{0,6},{1,7},{2,4},{3,5},{4,2},{5,3},{6,0},{7,1},{8,14},{9,15},{10,... | collective-permute-start | bytes 737288 | tf_op jit(solution)/shard_map/cond/branch_0_fun/ppermute | solution.py:35
  13.4 0.4 collective-permute-start.1
  13.8 0.1 collective-permute-start.2
  14.0 1.6 %collective-permute-start.3 = (bf16[192,640]{1,0:T(8,128)(2,1)S(1)}, bf16[192,640]{1,0:T(8,128)(2,1)S(1)}, u32[]{:S(2)}, u32[]{:S(2)}) collective-permute-start(bf16[192,640]{1,0:T(8,128)(2,1)S(1)} %get-tuple-element.89), channel_id=1, source_target_pairs={{0,5},{1,4},{2,7},{3,6},{4,1},{5,0},{6,3},{7,2},{8,13},{9,12},{10,... | collective-permute-start | bytes 737288 | tf_op jit(solution)/shard_map/cond/branch_0_fun/ppermute | solution.py:35
  15.5 2.5 %norm.7 = (bf16[192,640]{1,0:T(8,128)(2,1)}, bf16[192,640]{1,0:T(8,128)(2,1)}, bf16[192,640]{1,0:T(8,128)(2,1)}, bf16[192,640]{1,0:T(8,128)(2,1)S(1)}) custom-call(s32[16]{0:T(128)S(1)} %copy-done.16, bf16[64,5120]{1,0:T(8,128)(2,1)S(1)} %copy-done, bf16[64,5120]{1,0:T(8,128)(2,1)S(1)} %copy-done.3, bf16[64,5120]{1,0:T(8,128)(2,1)S(1)} %copy-done.6, ...), custom_call_target="tpu_custom_call" | custom-call | flops 3932160 | bytes 2621440 | tf_op jit(solution)/shard_map/cond/branch_0_fun/norm/pallas_call | solution.py:287
  18.0 21.0 %collective-permute-done.refs_0_ = bf16[192,640]{1,0:T(8,128)(2,1)S(1)} collective-permute-done((bf16[192,640]{1,0:T(8,128)(2,1)S(1)}, bf16[192,640]{1,0:T(8,128)(2,1)S(1)}, u32[]{:S(2)}, u32[]{:S(2)}) %collective-permute-start) | collective-permute-done | bytes 245792 | tf_op jit(solution)/shard_map/cond/branch_0_fun/ppermute | solution.py:35
  39.1 1.5 %collective-permute-start.4 = (bf16[192,640]{1,0:T(8,128)(2,1)}, bf16[192,640]{1,0:T(8,128)(2,1)S(1)}, u32[]{:S(2)}, u32[]{:S(2)}) collective-permute-start(bf16[192,640]{1,0:T(8,128)(2,1)} %get-tuple-element.90), channel_id=1, source_target_pairs={{0,2},{1,3},{2,0},{3,1},{4,6},{5,7},{6,4},{7,5},{8,10},{9,11},{10,... | collective-permute-start | bytes 737288 | tf_op jit(solution)/shard_map/cond/branch_0_fun/ppermute | solution.py:35
  40.6 3.8 %collective-permute-done.1.refs_1_ = bf16[192,640]{1,0:T(8,128)(2,1)S(1)} collective-permute-done((bf16[192,640]{1,0:T(8,128)(2,1)S(1)}, bf16[192,640]{1,0:T(8,128)(2,1)S(1)}, u32[]{:S(2)}, u32[]{:S(2)}) %collective-permute-start.1) | collective-permute-done | bytes 245792 | tf_op jit(solution)/shard_map/cond/branch_0_fun/ppermute | solution.py:35
  44.4 5.3 %collective-permute-done.2.refs_2_ = bf16[192,640]{1,0:T(8,128)(2,1)S(1)} collective-permute-done((bf16[192,640]{1,0:T(8,128)(2,1)S(1)}, bf16[192,640]{1,0:T(8,128)(2,1)S(1)}, u32[]{:S(2)}, u32[]{:S(2)}) %collective-permute-start.2) | collective-permute-done | bytes 245792 | tf_op jit(solution)/shard_map/cond/branch_0_fun/ppermute | solution.py:35
  51.6 0.8 %dynamic_slice.6.refs_9_ = bf16[1,640]{1,0:T(2,128)(2,1)S(1)} dynamic-slice(bf16[50,5120]{1,0:T(8,128)(2,1)} %get-tuple-element.96, s32[]{:T(128)S(6)} %select_n.24, s32[]{:T(128)S(6)} %select_n.26), dynamic_slice_sizes={1,640} | dynamic-slice | bytes 2564 | tf_op jit(solution)/shard_map/cond/branch_0_fun/dynamic_slice | solution.py:296
  52.4 1.4 %collective-permute-done.3.refs_3_ = bf16[192,640]{1,0:T(8,128)(2,1)S(1)} collective-permute-done((bf16[192,640]{1,0:T(8,128)(2,1)S(1)}, bf16[192,640]{1,0:T(8,128)(2,1)S(1)}, u32[]{:S(2)}, u32[]{:S(2)}) %collective-permute-start.3) | collective-permute-done | bytes 245792 | tf_op jit(solution)/shard_map/cond/branch_0_fun/ppermute | solution.py:35
  53.8 3.5 %collective-permute-done.7.refs_8_ = bf16[432,1280]{1,0:T(8,128)(2,1)} collective-permute-done((bf16[432,1280]{1,0:T(8,128)(2,1)S(1)}, bf16[432,1280]{1,0:T(8,128)(2,1)}, u32[]{:S(2)}, u32[]{:S(2)}) %collective-permute-start.7) | collective-permute-done | bytes 1105952 | tf_op jit(solution)/shard_map/cond/branch_0_fun/ppermute | solution.py:39
  57.3 5.3 %attend.3 = (bf16[64,640]{1,0:T(8,128)(2,1)S(1)}, bf16[64,640]{1,0:T(8,128)(2,1)S(1)}, bf16[64,640]{1,0:T(8,128)(2,1)S(1)}, bf16[64,640]{1,0:T(8,128)(2,1)S(1)},...) custom-call(s32[16]{0:T(128)S(1)} %copy-done.16, ...), custom_call_target="tpu_custom_call" | custom-call | flops 1342177280 | bytes 5242880 | tf_op jit(solution)/shard_map/cond/branch_0_fun/attend/pallas_call | solution.py:301
  62.6 1.5 %collective-permute-start.10 = (bf16[64,640]{1,0:T(8,128)(2,1)S(1)}, bf16[64,640]{1,0:T(8,128)(2,1)S(1)}, u32[]{:S(2)}, u32[]{:S(2)}) collective-permute-start(bf16[64,640]{1,0:T(8,128)(2,1)S(1)} %get-tuple-element.101), channel_id=1, source_target_pairs={{0,6},{1,7},{2,4},{3,5},{4,2},{5,3},{6,0},{7,1},{8,14},{9,15},{10,... | collective-permute-start | bytes 245768 | tf_op jit(solution)/shard_map/cond/branch_0_fun/ppermute | solution.py:35
  64.1 0.9 %collective-permute-start.11 = (bf16[64,640]{1,0:T(8,128)(2,1)S(1)}, bf16[64,640]{1,0:T(8,128)(2,1)S(1)}, u32[]{:S(2)}, u32[]{:S(2)}) collective-permute-start(bf16[64,640]{1,0:T(8,128)(2,1)S(1)} %get-tuple-element.102), channel_id=1, source_target_pairs={{0,7},{1,6},{2,5},{3,4},{4,3},{5,2},{6,1},{7,0},{8,15},{9,14},{10,... | collective-permute-start | bytes 245768 | tf_op jit(solution)/shard_map/cond/branch_0_fun/ppermute | solution.py:35
  65.0 1.5 %collective-permute-start.12 = (bf16[64,640]{1,0:T(8,128)(2,1)S(1)}, bf16[64,640]{1,0:T(8,128)(2,1)S(1)}, u32[]{:S(2)}, u32[]{:S(2)}) collective-permute-start(bf16[64,640]{1,0:T(8,128)(2,1)S(1)} %get-tuple-element.103), channel_id=1, source_target_pairs={{0,4},{1,5},{2,6},{3,7},{4,0},{5,1},{6,2},{7,3},{8,12},{9,13},{10,... | collective-permute-start | bytes 245768 | tf_op jit(solution)/shard_map/cond/branch_0_fun/ppermute | solution.py:35
  66.5 0.5 collective-permute-start.13
  67.0 1.4 %collective-permute-start.14 = (bf16[64,640]{1,0:T(8,128)(2,1)S(1)}, bf16[64,640]{1,0:T(8,128)(2,1)S(1)}, u32[]{:S(2)}, u32[]{:S(2)}) collective-permute-start(bf16[64,640]{1,0:T(8,128)(2,1)S(1)} %get-tuple-element.105), channel_id=1, source_target_pairs={{0,2},{1,3},{2,0},{3,1},{4,6},{5,7},{6,4},{7,5},{8,10},{9,11},{10,... | collective-permute-start | bytes 245768 | tf_op jit(solution)/shard_map/cond/branch_0_fun/ppermute | solution.py:35
  68.4 0.1 collective-permute-start.8
  68.5 1.2 %collective-permute-done.11.refs_3_ = bf16[64,640]{1,0:T(8,128)(2,1)S(1)} collective-permute-done((bf16[64,640]{1,0:T(8,128)(2,1)S(1)}, bf16[64,640]{1,0:T(8,128)(2,1)S(1)}, u32[]{:S(2)}, u32[]{:S(2)}) %collective-permute-start.11) | collective-permute-done | bytes 81952 | tf_op jit(solution)/shard_map/cond/branch_0_fun/ppermute | solution.py:35
  69.7 0.7 collective-permute-start.9
  70.4 1.2 %cache.3 = (bf16[1,512,640]{2,1,0:T(8,128)(2,1)}, bf16[1,512,640]{2,1,0:T(8,128)(2,1)}) custom-call(bf16[192,640]{1,0:T(8,128)(2,1)S(1)} %collective-permute-done.refs_0_, bf16[192,640]{1,0:T(8,128)(2,1)S(1)} %collective-permute-done.1.refs_1_, bf16[192,640]{1,0:T(8,128)(2,1)S(1)} %collective-permute-done.2.refs_2_, ...), custom_call_target="tpu_custom_call" | custom-call | bytes 2621440 | tf_op jit(solution)/shard_map/cond/branch_0_fun/cache/pallas_call | solution.py:317
  71.6 0.7 collective-permute-done.12.refs_4_
  72.3 0.7 collective-permute-done.8.refs_0_
  73.0 0.1 collect.3
  73.3 0.8 %copy-done.9 = bf16[64,5120]{1,0:T(8,128)(2,1)} copy-done((bf16[64,5120]{1,0:T(8,128)(2,1)}, bf16[64,5120]{1,0:T(8,128)(2,1)S(1)}, u32[]{:S(2)}) %copy-start.9) | copy-done | bytes 655384
  (27 shorter events, 0.1 us)
Async XLA Ops:
  2.5 6.5 %copy-start.10 = (bf16[5120]{0:T(1024)(128)(2,1)S(1)}, bf16[5120]{0:T(1024)(128)(2,1)}, u32[]{:S(2)}) copy-start(bf16[5120]{0:T(1024)(128)(2,1)} %get-tuple-element.83) | copy-start | bytes 30724 | tf_op jit(solution)/shard_map/cond
  2.5 6.5 %copy-start.13 = (bf16[5120]{0:T(1024)(128)(2,1)S(1)}, bf16[5120]{0:T(1024)(128)(2,1)}, u32[]{:S(2)}) copy-start(bf16[5120]{0:T(1024)(128)(2,1)} %get-tuple-element.84) | copy-start | bytes 30724 | tf_op jit(solution)/shard_map/cond
  2.5 6.5 %copy-start = (bf16[64,5120]{1,0:T(8,128)(2,1)S(1)}, bf16[64,5120]{1,0:T(8,128)(2,1)}, u32[]{:S(2)}) copy-start(bf16[64,5120]{1,0:T(8,128)(2,1)} %get-tuple-element.80.q) | copy-start | bytes 1966084 | tf_op jit(solution)/shard_map/cond
  2.6 6.5 %copy-start.3 = (bf16[64,5120]{1,0:T(8,128)(2,1)S(1)}, bf16[64,5120]{1,0:T(8,128)(2,1)}, u32[]{:S(2)}) copy-start(bf16[64,5120]{1,0:T(8,128)(2,1)} %get-tuple-element.81.k) | copy-start | bytes 1966084 | tf_op jit(solution)/shard_map/cond
  2.6 6.5 %copy-start.6 = (bf16[64,5120]{1,0:T(8,128)(2,1)S(1)}, bf16[64,5120]{1,0:T(8,128)(2,1)}, u32[]{:S(2)}) copy-start(bf16[64,5120]{1,0:T(8,128)(2,1)} %get-tuple-element.82.v) | copy-start | bytes 1966084 | tf_op jit(solution)/shard_map/cond
  2.6 6.5 %copy-start.16 = (s32[16]{0:T(128)S(1)}, s32[16]{0:T(128)}, u32[]{:S(2)}) copy-start(s32[16]{0:T(128)} %get-tuple-element.78.assign) | copy-start | bytes 196 | tf_op jit(solution)/shard_map/cond
  2.6 6.5 %copy-start.19 = (f32[1,128]{1,0:T(1,128)S(1)}, f32[1,128]{1,0:T(1,128)}, u32[]{:S(2)}) copy-start(f32[1,128]{1,0:T(1,128)} %get-tuple-element.85.steps) | copy-start | bytes 1540 | tf_op jit(solution)/shard_map/cond
  4.9 52.4 %collective-permute-start.7 = (bf16[432,1280]{1,0:T(8,128)(2,1)S(1)}, bf16[432,1280]{1,0:T(8,128)(2,1)}, u32[]{:S(2)}, u32[]{:S(2)}) collective-permute-start(bf16[432,1280]{1,0:T(8,128)(2,1)S(1)} %compact.3), channel_id=1, source_target_pairs={{0,8},{1,9},{2,10},{3,11},{4,12},{5,13},{6,14},{7,15},{8,0},{9,1},... | collective-permute-start | bytes 3317768 | tf_op jit(solution)/shard_map/cond/branch_0_fun/ppermute | solution.py:39
  10.8 46.5 %copy-start.22 = (s32[16]{0:T(128)S(1)}, s32[16]{0:T(128)}, u32[]{:S(2)}) copy-start(s32[16]{0:T(128)} %get-tuple-element.79.counts) | copy-start | bytes 196 | tf_op jit(solution)/shard_map/cond
  10.8 28.3 %collective-permute-start = (bf16[192,640]{1,0:T(8,128)(2,1)S(1)}, bf16[192,640]{1,0:T(8,128)(2,1)S(1)}, u32[]{:S(2)}, u32[]{:S(2)}) collective-permute-start(bf16[192,640]{1,0:T(8,128)(2,1)S(1)} %get-tuple-element.86), channel_id=1, source_target_pairs={{0,6},{1,7},{2,4},{3,5},{4,2},{5,3},{6,0},{7,1},{8,14},{9,15},{10,... | collective-permute-start | bytes 737288 | tf_op jit(solution)/shard_map/cond/branch_0_fun/ppermute | solution.py:35
  13.4 31.0 %collective-permute-start.1 = (bf16[192,640]{1,0:T(8,128)(2,1)S(1)}, bf16[192,640]{1,0:T(8,128)(2,1)S(1)}, u32[]{:S(2)}, u32[]{:S(2)}) collective-permute-start(bf16[192,640]{1,0:T(8,128)(2,1)S(1)} %get-tuple-element.87), channel_id=1, source_target_pairs={{0,4},{1,5},{2,6},{3,7},{4,0},{5,1},{6,2},{7,3},{8,12},{9,13},{10,... | collective-permute-start | bytes 737288 | tf_op jit(solution)/shard_map/cond/branch_0_fun/ppermute | solution.py:35
  13.8 35.9 %collective-permute-start.2 = (bf16[192,640]{1,0:T(8,128)(2,1)S(1)}, bf16[192,640]{1,0:T(8,128)(2,1)S(1)}, u32[]{:S(2)}, u32[]{:S(2)}) collective-permute-start(bf16[192,640]{1,0:T(8,128)(2,1)S(1)} %get-tuple-element.88), channel_id=1, source_target_pairs={{0,7},{1,6},{2,5},{3,4},{4,3},{5,2},{6,1},{7,0},{8,15},{9,14},{10,... | collective-permute-start | bytes 737288 | tf_op jit(solution)/shard_map/cond/branch_0_fun/ppermute | solution.py:35
  14.0 39.8 %collective-permute-start.3 = (bf16[192,640]{1,0:T(8,128)(2,1)S(1)}, bf16[192,640]{1,0:T(8,128)(2,1)S(1)}, u32[]{:S(2)}, u32[]{:S(2)}) collective-permute-start(bf16[192,640]{1,0:T(8,128)(2,1)S(1)} %get-tuple-element.89), channel_id=1, source_target_pairs={{0,5},{1,4},{2,7},{3,6},{4,1},{5,0},{6,3},{7,2},{8,13},{9,12},{10,... | collective-permute-start | bytes 737288 | tf_op jit(solution)/shard_map/cond/branch_0_fun/ppermute | solution.py:35
  39.1 14.7 %collective-permute-start.4 = (bf16[192,640]{1,0:T(8,128)(2,1)}, bf16[192,640]{1,0:T(8,128)(2,1)S(1)}, u32[]{:S(2)}, u32[]{:S(2)}) collective-permute-start(bf16[192,640]{1,0:T(8,128)(2,1)} %get-tuple-element.90), channel_id=1, source_target_pairs={{0,2},{1,3},{2,0},{3,1},{4,6},{5,7},{6,4},{7,5},{8,10},{9,11},{10,... | collective-permute-start | bytes 737288 | tf_op jit(solution)/shard_map/cond/branch_0_fun/ppermute | solution.py:35
  44.4 9.4 %collective-permute-start.5 = (bf16[192,640]{1,0:T(8,128)(2,1)}, bf16[192,640]{1,0:T(8,128)(2,1)S(1)}, u32[]{:S(2)}, u32[]{:S(2)}) collective-permute-start(bf16[192,640]{1,0:T(8,128)(2,1)} %get-tuple-element.91), channel_id=1, source_target_pairs={{0,3},{1,2},{2,1},{3,0},{4,7},{5,6},{6,5},{7,4},{8,11},{9,10},{10,... | collective-permute-start | bytes 737288 | tf_op jit(solution)/shard_map/cond/branch_0_fun/ppermute | solution.py:35
  49.7 4.1 %collective-permute-start.6 = (bf16[192,640]{1,0:T(8,128)(2,1)}, bf16[192,640]{1,0:T(8,128)(2,1)S(1)}, u32[]{:S(2)}, u32[]{:S(2)}) collective-permute-start(bf16[192,640]{1,0:T(8,128)(2,1)} %get-tuple-element.92), channel_id=1, source_target_pairs={{0,1},{1,0},{2,3},{3,2},{4,5},{5,4},{6,7},{7,6},{8,9},{9,8},{10,11... | collective-permute-start | bytes 737288 | tf_op jit(solution)/shard_map/cond/branch_0_fun/ppermute | solution.py:35
  62.6 5.9 %collective-permute-start.10 = (bf16[64,640]{1,0:T(8,128)(2,1)S(1)}, bf16[64,640]{1,0:T(8,128)(2,1)S(1)}, u32[]{:S(2)}, u32[]{:S(2)}) collective-permute-start(bf16[64,640]{1,0:T(8,128)(2,1)S(1)} %get-tuple-element.101), channel_id=1, source_target_pairs={{0,6},{1,7},{2,4},{3,5},{4,2},{5,3},{6,0},{7,1},{8,14},{9,15},{10,... | collective-permute-start | bytes 245768 | tf_op jit(solution)/shard_map/cond/branch_0_fun/ppermute | solution.py:35
  64.1 5.6 %collective-permute-start.11 = (bf16[64,640]{1,0:T(8,128)(2,1)S(1)}, bf16[64,640]{1,0:T(8,128)(2,1)S(1)}, u32[]{:S(2)}, u32[]{:S(2)}) collective-permute-start(bf16[64,640]{1,0:T(8,128)(2,1)S(1)} %get-tuple-element.102), channel_id=1, source_target_pairs={{0,7},{1,6},{2,5},{3,4},{4,3},{5,2},{6,1},{7,0},{8,15},{9,14},{10,... | collective-permute-start | bytes 245768 | tf_op jit(solution)/shard_map/cond/branch_0_fun/ppermute | solution.py:35
  65.0 7.3 %collective-permute-start.12 = (bf16[64,640]{1,0:T(8,128)(2,1)S(1)}, bf16[64,640]{1,0:T(8,128)(2,1)S(1)}, u32[]{:S(2)}, u32[]{:S(2)}) collective-permute-start(bf16[64,640]{1,0:T(8,128)(2,1)S(1)} %get-tuple-element.103), channel_id=1, source_target_pairs={{0,4},{1,5},{2,6},{3,7},{4,0},{5,1},{6,2},{7,3},{8,12},{9,13},{10,... | collective-permute-start | bytes 245768 | tf_op jit(solution)/shard_map/cond/branch_0_fun/ppermute | solution.py:35
  66.5 5.8 %collective-permute-start.13 = (bf16[64,640]{1,0:T(8,128)(2,1)S(1)}, bf16[64,640]{1,0:T(8,128)(2,1)S(1)}, u32[]{:S(2)}, u32[]{:S(2)}) collective-permute-start(bf16[64,640]{1,0:T(8,128)(2,1)S(1)} %get-tuple-element.104), channel_id=1, source_target_pairs={{0,5},{1,4},{2,7},{3,6},{4,1},{5,0},{6,3},{7,2},{8,13},{9,12},{10,... | collective-permute-start | bytes 245768 | tf_op jit(solution)/shard_map/cond/branch_0_fun/ppermute | solution.py:35
  67.0 5.3 %collective-permute-start.14 = (bf16[64,640]{1,0:T(8,128)(2,1)S(1)}, bf16[64,640]{1,0:T(8,128)(2,1)S(1)}, u32[]{:S(2)}, u32[]{:S(2)}) collective-permute-start(bf16[64,640]{1,0:T(8,128)(2,1)S(1)} %get-tuple-element.105), channel_id=1, source_target_pairs={{0,2},{1,3},{2,0},{3,1},{4,6},{5,7},{6,4},{7,5},{8,10},{9,11},{10,... | collective-permute-start | bytes 245768 | tf_op jit(solution)/shard_map/cond/branch_0_fun/ppermute | solution.py:35
  68.4 4.6 %collective-permute-start.8 = (bf16[64,640]{1,0:T(8,128)(2,1)S(1)}, bf16[64,640]{1,0:T(8,128)(2,1)S(1)}, u32[]{:S(2)}, u32[]{:S(2)}) collective-permute-start(bf16[64,640]{1,0:T(8,128)(2,1)S(1)} %get-tuple-element.99), channel_id=1, source_target_pairs={{0,3},{1,2},{2,1},{3,0},{4,7},{5,6},{6,5},{7,4},{8,11},{9,10},{10,... | collective-permute-start | bytes 245768 | tf_op jit(solution)/shard_map/cond/branch_0_fun/ppermute | solution.py:35
  69.7 3.3 %collective-permute-start.9 = (bf16[64,640]{1,0:T(8,128)(2,1)S(1)}, bf16[64,640]{1,0:T(8,128)(2,1)S(1)}, u32[]{:S(2)}, u32[]{:S(2)}) collective-permute-start(bf16[64,640]{1,0:T(8,128)(2,1)S(1)} %get-tuple-element.100), channel_id=1, source_target_pairs={{0,1},{1,0},{2,3},{3,2},{4,5},{5,4},{6,7},{7,6},{8,9},{9,8},{10,11... | collective-permute-start | bytes 245768 | tf_op jit(solution)/shard_map/cond/branch_0_fun/ppermute | solution.py:35
  73.3 0.8 %copy-start.9 = (bf16[64,5120]{1,0:T(8,128)(2,1)}, bf16[64,5120]{1,0:T(8,128)(2,1)S(1)}, u32[]{:S(2)}) copy-start(bf16[64,5120]{1,0:T(8,128)(2,1)S(1)} %get-tuple-element.174) | copy-start | bytes 1966084

commit v2 on v1

--- a/solution.py
+++ b/solution.py
@@ -254,7 +254,7 @@
     heads = wide // HEAD
     order = [6, 4, 7, 5, 2, 3, 1, 0]
     sizes = [block_rows * n // 32 for n in (27, 28, 32)] if blocks == 2 else [block_rows]
-    rare = sizes[2:]
+    rare = sizes[3:]
 
     (which,) = call(
         functools.partial(choose_kernel, slots, blocks, sizes),

time: 74.4 us -> 74.4 us (level)
  no operation moved by 1% of the time
where the time goes in v2:
time: 74.4 us; the launch traced here: 74.2 us
  waiting for transfers between devices  37.6 us (51%)
  starting transfers between devices  17 us (23%)
  Pallas kernels  14.2 us (19%)
  loops' own time  2.35 us (3%)
  local copies, waits for them, and re-layouts  1.7 us (2%)
  between operations  1.31 us (2%)
    ppermute x14, waiting for transfers between devices, to_partner(): return lax.ppermute(value, 'seq', [(i, i ^ distance) for i in range(size)])  34.1 us
    ppermute x14, starting transfers between devices, to_partner(): return lax.ppermute(value, 'seq', [(i, i ^ distance) for i in range(size)])  12.9 us
    pallas_call x1, Pallas kernels, step(): call(functools.partial(attend_kernel, order, tok, blocks, heads, rows in...  5.26 us
    pallas_call x2, Pallas kernels, run(): call(functools.partial(norm_kernel, slots, part, heads), 'norm', [SMEM] +...  4.2 us
    ppermute x1, starting transfers between devices, to_block(): lax.ppermute(value, 'seq', [(i, (i + distance) % size) for i in range(siz...  4.1 us
    ppermute x1, waiting for transfers between devices, to_block(): lax.ppermute(value, 'seq', [(i, (i + distance) % size) for i in range(siz...  3.49 us
    another operation x1, loops' own time, body(): lax.switch(which[0], [functools.partial(run, rows) for rows in sizes], op...  2.35 us
    pallas_call x1, Pallas kernels, run(): call(functools.partial(compact_kernel, slots, tok), 'compact', [SMEM] * 2...  2.28 us
  transfers between devices with their start and end apart: 15, of which 8 were waited for; matrix products, arithmetic and copies ran while one was open for 1% of the time, Pallas kernels for 7%

profile of v2, /device:TPU:0, one launch (start us, length us, event | category | flops | bytes accessed | tf_op | source)
XLA Modules:
  0.0 74.2 jit_solution(3100676196034319263)
XLA Ops:
  0.6 1.2 %choose.1 = s32[1]{0:T(128)} custom-call(s32[16]{0:T(128)} %assign.1, s32[16]{0:T(128)} %counts.1), custom_call_target="tpu_custom_call" | custom-call | bytes 5242880 | tf_op jit(solution)/shard_map/choose/pallas_call | solution.py:259
  2.5 70.8 %conditional.1 = (bf16[1,512,640]{2,1,0:T(8,128)(2,1)}, bf16[1,512,640]{2,1,0:T(8,128)(2,1)}, bf16[64,5120]{1,0:T(8,128)(2,1)S(1)}) conditional(s32[]{:T(128)} %bitcast.3, (bf16[5120]{0:T(1024)(128)(2,1)}, bf16[5120]{0:T(1024)(128)(2,1)}, s32[16]{0:T(128)}, bf16[64,5120]{1,0:T(8,128)(2,1)}, bf16[64,5120]{1,0:T(8,128)(2,1)}, ...), branch_computations={%region_0.1_spmd, %region_1.2_spmd, %region_2.3_spmd} | conditional | flops 2021130240 | bytes 39450632 | solution.py:348
  2.6 0.0 copy-start.19
  2.6 2.3 %compact.3 = bf16[432,1280]{1,0:T(8,128)(2,1)S(1)} custom-call(s32[16]{0:T(128)} %get-tuple-element.78.assign, s32[16]{0:T(128)} %get-tuple-element.79.counts, bf16[1,512,640]{2,1,0:T(8,128)(2,1)} %get-tuple-element.94.keys, bf16[1,512,640]{2,1,0:T(8,128)(2,1)} %get-tuple-element.95.values), custom_call_target="tpu_custom_call" | custom-call | flops 566231040 | bytes 2416640 | tf_op jit(solution)/shard_map/cond/branch_0_fun/compact/pallas_call | solution.py:276
  4.9 4.1 %collective-permute-start.7 = (bf16[432,1280]{1,0:T(8,128)(2,1)S(1)}, bf16[432,1280]{1,0:T(8,128)(2,1)}, u32[]{:S(2)}, u32[]{:S(2)}) collective-permute-start(bf16[432,1280]{1,0:T(8,128)(2,1)S(1)} %compact.3), channel_id=1, source_target_pairs={{0,8},{1,9},{2,10},{3,11},{4,12},{5,13},{6,14},{7,15},{8,0},{9,1},... | collective-permute-start | bytes 3317768 | tf_op jit(solution)/shard_map/cond/branch_0_fun/ppermute | solution.py:39
  9.1 1.7 %norm.6 = (bf16[192,640]{1,0:T(8,128)(2,1)S(1)}, bf16[192,640]{1,0:T(8,128)(2,1)S(1)}, bf16[192,640]{1,0:T(8,128)(2,1)S(1)}, bf16[192,640]{1,0:T(8,128)(2,1)S(1)}) custom-call(s32[16]{0:T(128)S(1)} %copy-done.16, bf16[64,5120]{1,0:T(8,128)(2,1)S(1)} %copy-done, bf16[64,5120]{1,0:T(8,128)(2,1)S(1)} %copy-done.3, bf16[64,5120]{1,0:T(8,128)(2,1)S(1)} %copy-done.6, ...), custom_call_target="tpu_custom_call" | custom-call | flops 3932160 | bytes 2621440 | tf_op jit(solution)/shard_map/cond/branch_0_fun/norm/pallas_call | solution.py:287
  10.8 2.6 %collective-permute-start = (bf16[192,640]{1,0:T(8,128)(2,1)S(1)}, bf16[192,640]{1,0:T(8,128)(2,1)S(1)}, u32[]{:S(2)}, u32[]{:S(2)}) collective-permute-start(bf16[192,640]{1,0:T(8,128)(2,1)S(1)} %get-tuple-element.86), channel_id=1, source_target_pairs={{0,6},{1,7},{2,4},{3,5},{4,2},{5,3},{6,0},{7,1},{8,14},{9,15},{10,... | collective-permute-start | bytes 737288 | tf_op jit(solution)/shard_map/cond/branch_0_fun/ppermute | solution.py:35
  13.4 0.4 collective-permute-start.1
  13.8 0.1 collective-permute-start.2
  14.0 1.6 %collective-permute-start.3 = (bf16[192,640]{1,0:T(8,128)(2,1)S(1)}, bf16[192,640]{1,0:T(8,128)(2,1)S(1)}, u32[]{:S(2)}, u32[]{:S(2)}) collective-permute-start(bf16[192,640]{1,0:T(8,128)(2,1)S(1)} %get-tuple-element.89), channel_id=1, source_target_pairs={{0,5},{1,4},{2,7},{3,6},{4,1},{5,0},{6,3},{7,2},{8,13},{9,12},{10,... | collective-permute-start | bytes 737288 | tf_op jit(solution)/shard_map/cond/branch_0_fun/ppermute | solution.py:35
  15.5 2.5 %norm.7 = (bf16[192,640]{1,0:T(8,128)(2,1)}, bf16[192,640]{1,0:T(8,128)(2,1)}, bf16[192,640]{1,0:T(8,128)(2,1)}, bf16[192,640]{1,0:T(8,128)(2,1)S(1)}) custom-call(s32[16]{0:T(128)S(1)} %copy-done.16, bf16[64,5120]{1,0:T(8,128)(2,1)S(1)} %copy-done, bf16[64,5120]{1,0:T(8,128)(2,1)S(1)} %copy-done.3, bf16[64,5120]{1,0:T(8,128)(2,1)S(1)} %copy-done.6, ...), custom_call_target="tpu_custom_call" | custom-call | flops 3932160 | bytes 2621440 | tf_op jit(solution)/shard_map/cond/branch_0_fun/norm/pallas_call | solution.py:287
  18.0 21.0 %collective-permute-done.refs_0_ = bf16[192,640]{1,0:T(8,128)(2,1)S(1)} collective-permute-done((bf16[192,640]{1,0:T(8,128)(2,1)S(1)}, bf16[192,640]{1,0:T(8,128)(2,1)S(1)}, u32[]{:S(2)}, u32[]{:S(2)}) %collective-permute-start) | collective-permute-done | bytes 245792 | tf_op jit(solution)/shard_map/cond/branch_0_fun/ppermute | solution.py:35
  39.1 1.5 %collective-permute-start.4 = (bf16[192,640]{1,0:T(8,128)(2,1)}, bf16[192,640]{1,0:T(8,128)(2,1)S(1)}, u32[]{:S(2)}, u32[]{:S(2)}) collective-permute-start(bf16[192,640]{1,0:T(8,128)(2,1)} %get-tuple-element.90), channel_id=1, source_target_pairs={{0,2},{1,3},{2,0},{3,1},{4,6},{5,7},{6,4},{7,5},{8,10},{9,11},{10,... | collective-permute-start | bytes 737288 | tf_op jit(solution)/shard_map/cond/branch_0_fun/ppermute | solution.py:35
  40.6 3.8 %collective-permute-done.1.refs_1_ = bf16[192,640]{1,0:T(8,128)(2,1)S(1)} collective-permute-done((bf16[192,640]{1,0:T(8,128)(2,1)S(1)}, bf16[192,640]{1,0:T(8,128)(2,1)S(1)}, u32[]{:S(2)}, u32[]{:S(2)}) %collective-permute-start.1) | collective-permute-done | bytes 245792 | tf_op jit(solution)/shard_map/cond/branch_0_fun/ppermute | solution.py:35
  44.4 5.3 %collective-permute-done.2.refs_2_ = bf16[192,640]{1,0:T(8,128)(2,1)S(1)} collective-permute-done((bf16[192,640]{1,0:T(8,128)(2,1)S(1)}, bf16[192,640]{1,0:T(8,128)(2,1)S(1)}, u32[]{:S(2)}, u32[]{:S(2)}) %collective-permute-start.2) | collective-permute-done | bytes 245792 | tf_op jit(solution)/shard_map/cond/branch_0_fun/ppermute | solution.py:35
  51.6 0.8 %dynamic_slice.6.refs_9_ = bf16[1,640]{1,0:T(2,128)(2,1)S(1)} dynamic-slice(bf16[50,5120]{1,0:T(8,128)(2,1)} %get-tuple-element.96, s32[]{:T(128)S(6)} %select_n.24, s32[]{:T(128)S(6)} %select_n.26), dynamic_slice_sizes={1,640} | dynamic-slice | bytes 2564 | tf_op jit(solution)/shard_map/cond/branch_0_fun/dynamic_slice | solution.py:296
  52.4 1.4 %collective-permute-done.3.refs_3_ = bf16[192,640]{1,0:T(8,128)(2,1)S(1)} collective-permute-done((bf16[192,640]{1,0:T(8,128)(2,1)S(1)}, bf16[192,640]{1,0:T(8,128)(2,1)S(1)}, u32[]{:S(2)}, u32[]{:S(2)}) %collective-permute-start.3) | collective-permute-done | bytes 245792 | tf_op jit(solution)/shard_map/cond/branch_0_fun/ppermute | solution.py:35
  53.8 3.5 %collective-permute-done.7.refs_8_ = bf16[432,1280]{1,0:T(8,128)(2,1)} collective-permute-done((bf16[432,1280]{1,0:T(8,128)(2,1)S(1)}, bf16[432,1280]{1,0:T(8,128)(2,1)}, u32[]{:S(2)}, u32[]{:S(2)}) %collective-permute-start.7) | collective-permute-done | bytes 1105952 | tf_op jit(solution)/shard_map/cond/branch_0_fun/ppermute | solution.py:39
  57.3 5.3 %attend.3 = (bf16[64,640]{1,0:T(8,128)(2,1)S(1)}, bf16[64,640]{1,0:T(8,128)(2,1)S(1)}, bf16[64,640]{1,0:T(8,128)(2,1)S(1)}, bf16[64,640]{1,0:T(8,128)(2,1)S(1)},...) custom-call(s32[16]{0:T(128)S(1)} %copy-done.16, ...), custom_call_target="tpu_custom_call" | custom-call | flops 1342177280 | bytes 5242880 | tf_op jit(solution)/shard_map/cond/branch_0_fun/attend/pallas_call | solution.py:301
  62.6 1.5 %collective-permute-start.10 = (bf16[64,640]{1,0:T(8,128)(2,1)S(1)}, bf16[64,640]{1,0:T(8,128)(2,1)S(1)}, u32[]{:S(2)}, u32[]{:S(2)}) collective-permute-start(bf16[64,640]{1,0:T(8,128)(2,1)S(1)} %get-tuple-element.101), channel_id=1, source_target_pairs={{0,6},{1,7},{2,4},{3,5},{4,2},{5,3},{6,0},{7,1},{8,14},{9,15},{10,... | collective-permute-start | bytes 245768 | tf_op jit(solution)/shard_map/cond/branch_0_fun/ppermute | solution.py:35
  64.1 0.9 %collective-permute-start.11 = (bf16[64,640]{1,0:T(8,128)(2,1)S(1)}, bf16[64,640]{1,0:T(8,128)(2,1)S(1)}, u32[]{:S(2)}, u32[]{:S(2)}) collective-permute-start(bf16[64,640]{1,0:T(8,128)(2,1)S(1)} %get-tuple-element.102), channel_id=1, source_target_pairs={{0,7},{1,6},{2,5},{3,4},{4,3},{5,2},{6,1},{7,0},{8,15},{9,14},{10,... | collective-permute-start | bytes 245768 | tf_op jit(solution)/shard_map/cond/branch_0_fun/ppermute | solution.py:35
  65.0 1.5 %collective-permute-start.12 = (bf16[64,640]{1,0:T(8,128)(2,1)S(1)}, bf16[64,640]{1,0:T(8,128)(2,1)S(1)}, u32[]{:S(2)}, u32[]{:S(2)}) collective-permute-start(bf16[64,640]{1,0:T(8,128)(2,1)S(1)} %get-tuple-element.103), channel_id=1, source_target_pairs={{0,4},{1,5},{2,6},{3,7},{4,0},{5,1},{6,2},{7,3},{8,12},{9,13},{10,... | collective-permute-start | bytes 245768 | tf_op jit(solution)/shard_map/cond/branch_0_fun/ppermute | solution.py:35
  66.5 0.5 collective-permute-start.13
  67.0 1.4 %collective-permute-start.14 = (bf16[64,640]{1,0:T(8,128)(2,1)S(1)}, bf16[64,640]{1,0:T(8,128)(2,1)S(1)}, u32[]{:S(2)}, u32[]{:S(2)}) collective-permute-start(bf16[64,640]{1,0:T(8,128)(2,1)S(1)} %get-tuple-element.105), channel_id=1, source_target_pairs={{0,2},{1,3},{2,0},{3,1},{4,6},{5,7},{6,4},{7,5},{8,10},{9,11},{10,... | collective-permute-start | bytes 245768 | tf_op jit(solution)/shard_map/cond/branch_0_fun/ppermute | solution.py:35
  68.4 0.1 collective-permute-start.8
  68.5 1.2 %collective-permute-done.11.refs_3_ = bf16[64,640]{1,0:T(8,128)(2,1)S(1)} collective-permute-done((bf16[64,640]{1,0:T(8,128)(2,1)S(1)}, bf16[64,640]{1,0:T(8,128)(2,1)S(1)}, u32[]{:S(2)}, u32[]{:S(2)}) %collective-permute-start.11) | collective-permute-done | bytes 81952 | tf_op jit(solution)/shard_map/cond/branch_0_fun/ppermute | solution.py:35
  69.7 0.7 collective-permute-start.9
  70.4 1.2 %cache.3 = (bf16[1,512,640]{2,1,0:T(8,128)(2,1)}, bf16[1,512,640]{2,1,0:T(8,128)(2,1)}) custom-call(bf16[192,640]{1,0:T(8,128)(2,1)S(1)} %collective-permute-done.refs_0_, bf16[192,640]{1,0:T(8,128)(2,1)S(1)} %collective-permute-done.1.refs_1_, bf16[192,640]{1,0:T(8,128)(2,1)S(1)} %collective-permute-done.2.refs_2_, ...), custom_call_target="tpu_custom_call" | custom-call | bytes 2621440 | tf_op jit(solution)/shard_map/cond/branch_0_fun/cache/pallas_call | solution.py:317
  71.6 0.7 collective-permute-done.12.refs_4_
  72.3 0.7 collective-permute-done.8.refs_0_
  73.0 0.1 collect.3
  73.3 0.8 %copy-done.9 = bf16[64,5120]{1,0:T(8,128)(2,1)} copy-done((bf16[64,5120]{1,0:T(8,128)(2,1)}, bf16[64,5120]{1,0:T(8,128)(2,1)S(1)}, u32[]{:S(2)}) %copy-start.9) | copy-done | bytes 655384
  (27 shorter events, 0.1 us)
Async XLA Ops:
  2.5 6.5 %copy-start.10 = (bf16[5120]{0:T(1024)(128)(2,1)S(1)}, bf16[5120]{0:T(1024)(128)(2,1)}, u32[]{:S(2)}) copy-start(bf16[5120]{0:T(1024)(128)(2,1)} %get-tuple-element.83) | copy-start | bytes 30724 | tf_op jit(solution)/shard_map/cond
  2.5 6.5 %copy-start.13 = (bf16[5120]{0:T(1024)(128)(2,1)S(1)}, bf16[5120]{0:T(1024)(128)(2,1)}, u32[]{:S(2)}) copy-start(bf16[5120]{0:T(1024)(128)(2,1)} %get-tuple-element.84) | copy-start | bytes 30724 | tf_op jit(solution)/shard_map/cond
  2.5 6.5 %copy-start = (bf16[64,5120]{1,0:T(8,128)(2,1)S(1)}, bf16[64,5120]{1,0:T(8,128)(2,1)}, u32[]{:S(2)}) copy-start(bf16[64,5120]{1,0:T(8,128)(2,1)} %get-tuple-element.80.q) | copy-start | bytes 1966084 | tf_op jit(solution)/shard_map/cond
  2.6 6.5 %copy-start.3 = (bf16[64,5120]{1,0:T(8,128)(2,1)S(1)}, bf16[64,5120]{1,0:T(8,128)(2,1)}, u32[]{:S(2)}) copy-start(bf16[64,5120]{1,0:T(8,128)(2,1)} %get-tuple-element.81.k) | copy-start | bytes 1966084 | tf_op jit(solution)/shard_map/cond
  2.6 6.5 %copy-start.6 = (bf16[64,5120]{1,0:T(8,128)(2,1)S(1)}, bf16[64,5120]{1,0:T(8,128)(2,1)}, u32[]{:S(2)}) copy-start(bf16[64,5120]{1,0:T(8,128)(2,1)} %get-tuple-element.82.v) | copy-start | bytes 1966084 | tf_op jit(solution)/shard_map/cond
  2.6 6.5 %copy-start.16 = (s32[16]{0:T(128)S(1)}, s32[16]{0:T(128)}, u32[]{:S(2)}) copy-start(s32[16]{0:T(128)} %get-tuple-element.78.assign) | copy-start | bytes 196 | tf_op jit(solution)/shard_map/cond
  2.6 6.5 %copy-start.19 = (f32[1,128]{1,0:T(1,128)S(1)}, f32[1,128]{1,0:T(1,128)}, u32[]{:S(2)}) copy-start(f32[1,128]{1,0:T(1,128)} %get-tuple-element.85.steps) | copy-start | bytes 1540 | tf_op jit(solution)/shard_map/cond
  4.9 52.4 %collective-permute-start.7 = (bf16[432,1280]{1,0:T(8,128)(2,1)S(1)}, bf16[432,1280]{1,0:T(8,128)(2,1)}, u32[]{:S(2)}, u32[]{:S(2)}) collective-permute-start(bf16[432,1280]{1,0:T(8,128)(2,1)S(1)} %compact.3), channel_id=1, source_target_pairs={{0,8},{1,9},{2,10},{3,11},{4,12},{5,13},{6,14},{7,15},{8,0},{9,1},... | collective-permute-start | bytes 3317768 | tf_op jit(solution)/shard_map/cond/branch_0_fun/ppermute | solution.py:39
  10.8 46.5 %copy-start.22 = (s32[16]{0:T(128)S(1)}, s32[16]{0:T(128)}, u32[]{:S(2)}) copy-start(s32[16]{0:T(128)} %get-tuple-element.79.counts) | copy-start | bytes 196 | tf_op jit(solution)/shard_map/cond
  10.8 28.3 %collective-permute-start = (bf16[192,640]{1,0:T(8,128)(2,1)S(1)}, bf16[192,640]{1,0:T(8,128)(2,1)S(1)}, u32[]{:S(2)}, u32[]{:S(2)}) collective-permute-start(bf16[192,640]{1,0:T(8,128)(2,1)S(1)} %get-tuple-element.86), channel_id=1, source_target_pairs={{0,6},{1,7},{2,4},{3,5},{4,2},{5,3},{6,0},{7,1},{8,14},{9,15},{10,... | collective-permute-start | bytes 737288 | tf_op jit(solution)/shard_map/cond/branch_0_fun/ppermute | solution.py:35
  13.4 31.0 %collective-permute-start.1 = (bf16[192,640]{1,0:T(8,128)(2,1)S(1)}, bf16[192,640]{1,0:T(8,128)(2,1)S(1)}, u32[]{:S(2)}, u32[]{:S(2)}) collective-permute-start(bf16[192,640]{1,0:T(8,128)(2,1)S(1)} %get-tuple-element.87), channel_id=1, source_target_pairs={{0,4},{1,5},{2,6},{3,7},{4,0},{5,1},{6,2},{7,3},{8,12},{9,13},{10,... | collective-permute-start | bytes 737288 | tf_op jit(solution)/shard_map/cond/branch_0_fun/ppermute | solution.py:35
  13.8 35.9 %collective-permute-start.2 = (bf16[192,640]{1,0:T(8,128)(2,1)S(1)}, bf16[192,640]{1,0:T(8,128)(2,1)S(1)}, u32[]{:S(2)}, u32[]{:S(2)}) collective-permute-start(bf16[192,640]{1,0:T(8,128)(2,1)S(1)} %get-tuple-element.88), channel_id=1, source_target_pairs={{0,7},{1,6},{2,5},{3,4},{4,3},{5,2},{6,1},{7,0},{8,15},{9,14},{10,... | collective-permute-start | bytes 737288 | tf_op jit(solution)/shard_map/cond/branch_0_fun/ppermute | solution.py:35
  14.0 39.8 %collective-permute-start.3 = (bf16[192,640]{1,0:T(8,128)(2,1)S(1)}, bf16[192,640]{1,0:T(8,128)(2,1)S(1)}, u32[]{:S(2)}, u32[]{:S(2)}) collective-permute-start(bf16[192,640]{1,0:T(8,128)(2,1)S(1)} %get-tuple-element.89), channel_id=1, source_target_pairs={{0,5},{1,4},{2,7},{3,6},{4,1},{5,0},{6,3},{7,2},{8,13},{9,12},{10,... | collective-permute-start | bytes 737288 | tf_op jit(solution)/shard_map/cond/branch_0_fun/ppermute | solution.py:35
  39.1 14.7 %collective-permute-start.4 = (bf16[192,640]{1,0:T(8,128)(2,1)}, bf16[192,640]{1,0:T(8,128)(2,1)S(1)}, u32[]{:S(2)}, u32[]{:S(2)}) collective-permute-start(bf16[192,640]{1,0:T(8,128)(2,1)} %get-tuple-element.90), channel_id=1, source_target_pairs={{0,2},{1,3},{2,0},{3,1},{4,6},{5,7},{6,4},{7,5},{8,10},{9,11},{10,... | collective-permute-start | bytes 737288 | tf_op jit(solution)/shard_map/cond/branch_0_fun/ppermute | solution.py:35
  44.4 9.4 %collective-permute-start.5 = (bf16[192,640]{1,0:T(8,128)(2,1)}, bf16[192,640]{1,0:T(8,128)(2,1)S(1)}, u32[]{:S(2)}, u32[]{:S(2)}) collective-permute-start(bf16[192,640]{1,0:T(8,128)(2,1)} %get-tuple-element.91), channel_id=1, source_target_pairs={{0,3},{1,2},{2,1},{3,0},{4,7},{5,6},{6,5},{7,4},{8,11},{9,10},{10,... | collective-permute-start | bytes 737288 | tf_op jit(solution)/shard_map/cond/branch_0_fun/ppermute | solution.py:35
  49.7 4.1 %collective-permute-start.6 = (bf16[192,640]{1,0:T(8,128)(2,1)}, bf16[192,640]{1,0:T(8,128)(2,1)S(1)}, u32[]{:S(2)}, u32[]{:S(2)}) collective-permute-start(bf16[192,640]{1,0:T(8,128)(2,1)} %get-tuple-element.92), channel_id=1, source_target_pairs={{0,1},{1,0},{2,3},{3,2},{4,5},{5,4},{6,7},{7,6},{8,9},{9,8},{10,11... | collective-permute-start | bytes 737288 | tf_op jit(solution)/shard_map/cond/branch_0_fun/ppermute | solution.py:35
  62.6 5.9 %collective-permute-start.10 = (bf16[64,640]{1,0:T(8,128)(2,1)S(1)}, bf16[64,640]{1,0:T(8,128)(2,1)S(1)}, u32[]{:S(2)}, u32[]{:S(2)}) collective-permute-start(bf16[64,640]{1,0:T(8,128)(2,1)S(1)} %get-tuple-element.101), channel_id=1, source_target_pairs={{0,6},{1,7},{2,4},{3,5},{4,2},{5,3},{6,0},{7,1},{8,14},{9,15},{10,... | collective-permute-start | bytes 245768 | tf_op jit(solution)/shard_map/cond/branch_0_fun/ppermute | solution.py:35
  64.1 5.6 %collective-permute-start.11 = (bf16[64,640]{1,0:T(8,128)(2,1)S(1)}, bf16[64,640]{1,0:T(8,128)(2,1)S(1)}, u32[]{:S(2)}, u32[]{:S(2)}) collective-permute-start(bf16[64,640]{1,0:T(8,128)(2,1)S(1)} %get-tuple-element.102), channel_id=1, source_target_pairs={{0,7},{1,6},{2,5},{3,4},{4,3},{5,2},{6,1},{7,0},{8,15},{9,14},{10,... | collective-permute-start | bytes 245768 | tf_op jit(solution)/shard_map/cond/branch_0_fun/ppermute | solution.py:35
  65.0 7.3 %collective-permute-start.12 = (bf16[64,640]{1,0:T(8,128)(2,1)S(1)}, bf16[64,640]{1,0:T(8,128)(2,1)S(1)}, u32[]{:S(2)}, u32[]{:S(2)}) collective-permute-start(bf16[64,640]{1,0:T(8,128)(2,1)S(1)} %get-tuple-element.103), channel_id=1, source_target_pairs={{0,4},{1,5},{2,6},{3,7},{4,0},{5,1},{6,2},{7,3},{8,12},{9,13},{10,... | collective-permute-start | bytes 245768 | tf_op jit(solution)/shard_map/cond/branch_0_fun/ppermute | solution.py:35
  66.5 5.8 %collective-permute-start.13 = (bf16[64,640]{1,0:T(8,128)(2,1)S(1)}, bf16[64,640]{1,0:T(8,128)(2,1)S(1)}, u32[]{:S(2)}, u32[]{:S(2)}) collective-permute-start(bf16[64,640]{1,0:T(8,128)(2,1)S(1)} %get-tuple-element.104), channel_id=1, source_target_pairs={{0,5},{1,4},{2,7},{3,6},{4,1},{5,0},{6,3},{7,2},{8,13},{9,12},{10,... | collective-permute-start | bytes 245768 | tf_op jit(solution)/shard_map/cond/branch_0_fun/ppermute | solution.py:35
  67.0 5.3 %collective-permute-start.14 = (bf16[64,640]{1,0:T(8,128)(2,1)S(1)}, bf16[64,640]{1,0:T(8,128)(2,1)S(1)}, u32[]{:S(2)}, u32[]{:S(2)}) collective-permute-start(bf16[64,640]{1,0:T(8,128)(2,1)S(1)} %get-tuple-element.105), channel_id=1, source_target_pairs={{0,2},{1,3},{2,0},{3,1},{4,6},{5,7},{6,4},{7,5},{8,10},{9,11},{10,... | collective-permute-start | bytes 245768 | tf_op jit(solution)/shard_map/cond/branch_0_fun/ppermute | solution.py:35
  68.4 4.6 %collective-permute-start.8 = (bf16[64,640]{1,0:T(8,128)(2,1)S(1)}, bf16[64,640]{1,0:T(8,128)(2,1)S(1)}, u32[]{:S(2)}, u32[]{:S(2)}) collective-permute-start(bf16[64,640]{1,0:T(8,128)(2,1)S(1)} %get-tuple-element.99), channel_id=1, source_target_pairs={{0,3},{1,2},{2,1},{3,0},{4,7},{5,6},{6,5},{7,4},{8,11},{9,10},{10,... | collective-permute-start | bytes 245768 | tf_op jit(solution)/shard_map/cond/branch_0_fun/ppermute | solution.py:35
  69.7 3.3 %collective-permute-start.9 = (bf16[64,640]{1,0:T(8,128)(2,1)S(1)}, bf16[64,640]{1,0:T(8,128)(2,1)S(1)}, u32[]{:S(2)}, u32[]{:S(2)}) collective-permute-start(bf16[64,640]{1,0:T(8,128)(2,1)S(1)} %get-tuple-element.100), channel_id=1, source_target_pairs={{0,1},{1,0},{2,3},{3,2},{4,5},{5,4},{6,7},{7,6},{8,9},{9,8},{10,11... | collective-permute-start | bytes 245768 | tf_op jit(solution)/shard_map/cond/branch_0_fun/ppermute | solution.py:35
  73.3 0.8 %copy-start.9 = (bf16[64,5120]{1,0:T(8,128)(2,1)}, bf16[64,5120]{1,0:T(8,128)(2,1)S(1)}, u32[]{:S(2)}) copy-start(bf16[64,5120]{1,0:T(8,128)(2,1)S(1)} %get-tuple-element.174) | copy-start | bytes 1966084
